TPU v7x, 256 devices: a whole 4x4x8 slice. The times are simulated.
256 devices in a mesh: date: 32 (over z_lo, x, core), strip: 8 (over z_hi, y).
Axes of the slice: x: 4, y: 4, z: 8 (z_hi: 2, z_lo: 4; z = z_hi * 4 + z_lo), core: 2. Of those that a mesh axis runs over, the one named last changes fastest.
Arguments:
- slc: bfloat16 [64, 2, 256, 1024], P('date', None, 'strip'), as said below
- partner: int32 [4, 32, 2], P(None, 'date'), may hold values from 0 to 1, each once within a row
- valid: int32 [4, 64, 2], P(None, 'date'), may hold values from 0 to 256, as said below
Outputs:
- coherence: float32 [4, 64, 256, 1024], P(None, 'date', 'strip')
- filtered: float32 [4, 64, 2, 256, 1024], P(None, 'date', None, 'strip')
Inputs may be any that keep to these rules, and one draw needn't show every extreme that they name: Each row partner[r, b, :] is a permutation of the 2 positions of a block. valid[r, i, 0] <= 128 < valid[r, i, 1]; date 0 is valid on all 256 rows in every round. `slc`: finite values.
All inputs are finite; a program needn't handle non-finite values.
Results may differ from a plain program's by a relative error of at most 0.0015.
Values may be sent and summed in bfloat16 or wider, within the bound.
A program may use at most 64 MiB of HBM per device.

v0:
```python
import functools
import math

import jax
import jax.numpy as jnp
import numpy as np
from jax import lax
from jax.experimental import pallas as pl
from jax.experimental.pallas import tpu as pltpu
from jax.sharding import PartitionSpec as P

F32 = jnp.float32
BF16 = jnp.bfloat16
MESH = pl.DeviceIdType.MESH

PATCH = 32
LOOK_A = 5
LOOK_R = 19
HALO = 2
LANES = 128
SUBS = 8
ROWS = 32
EXT = ROWS + 2 * HALO
EDGE = HALO * SUBS
BODY = ROWS * SUBS
FULL = EXT * SUBS
TINY = 1.2e-38

BOX_SCALE = 1.0 / 128.0
BOX_RATIO = LOOK_A * LOOK_R / 128.0


def split_np(table):
    high = table.astype(np.float32).astype(jnp.bfloat16)
    low = (table - high.astype(np.float64)).astype(np.float32).astype(jnp.bfloat16)
    return high, low


def make_tables():
    lane = np.arange(LANES)
    reach = LOOK_R // 2
    centre = np.abs(lane[:, None] - lane[None, :]) <= reach
    to_next = np.abs(lane[None, :] + LANES - lane[:, None]) <= reach
    to_previous = np.abs(lane[None, :] - LANES - lane[:, None]) <= reach
    box = np.concatenate([centre, to_next | to_previous], 1) * BOX_SCALE
    box = np.concatenate([box, box], 0)

    same = lane[:, None] // PATCH == lane[None, :] // PATCH
    angle = (lane[:, None] % PATCH) * (lane[None, :] % PATCH) % PATCH * (2 * math.pi / PATCH)
    cos = np.where(same, np.cos(angle), 0.0)
    sin = np.where(same, np.sin(angle), 0.0)
    forward = np.block([[cos, -sin], [sin, cos]]) / (BOX_RATIO * PATCH * PATCH)
    inverse = np.block([[cos, sin], [-sin, cos]])
    apart = (lane[:, None] - lane[None, :]) % PATCH
    near = same & ((apart <= 1) | (apart == PATCH - 1))

    def triple(table):
        high, low = split_np(table)
        return np.concatenate([high, high, low], 0)

    def twice(table):
        return np.concatenate([table, table], 0).astype(np.float32).astype(jnp.bfloat16)

    return (
        box.astype(np.float32).astype(jnp.bfloat16),
        triple(forward),
        triple(inverse),
        twice(near),
        twice(same),
    )


def cmul(value, angle):
    re, im = value
    c, s = math.cos(angle), math.sin(angle)
    quarter = round(angle / (math.pi / 4), 9)
    if quarter == int(quarter):
        turn = int(quarter) % 8
        h = math.sqrt(0.5)
        return [
            lambda: (re, im),
            lambda: ((re - im) * h, (re + im) * h),
            lambda: (-im, re),
            lambda: (-(re + im) * h, (re - im) * h),
            lambda: (-re, -im),
            lambda: ((im - re) * h, -(re + im) * h),
            lambda: (im, -re),
            lambda: ((re + im) * h, (im - re) * h),
        ][turn]()
    return re * c - im * s, re * s + im * c


def cadd(a, b):
    return a[0] + b[0], a[1] + b[1]


def csub(a, b):
    return a[0] - b[0], a[1] - b[1]


def add_turned(a, b, sign):
    if sign > 0:
        return a[0] - b[1], a[1] + b[0]
    return a[0] + b[1], a[1] - b[0]


def dft4(x, sign):
    s0, d0 = cadd(x[0], x[2]), csub(x[0], x[2])
    s1, d1 = cadd(x[1], x[3]), csub(x[1], x[3])
    return [cadd(s0, s1), add_turned(d0, d1, sign), csub(s0, s1), add_turned(d0, d1, -sign)]


def dft8(x, sign):
    even = dft4(x[0::2], sign)
    odd = dft4(x[1::2], sign)
    out = [None] * 8
    h = math.sqrt(0.5)
    for k in range(4):
        if k == 2:
            out[2] = add_turned(even[2], odd[2], sign)
            out[6] = add_turned(even[2], odd[2], -sign)
            continue
        turned = odd[k] if k == 0 else cmul(odd[k], sign * k * math.pi / 4)
        out[k] = cadd(even[k], turned)
        out[k + 4] = csub(even[k], turned)
    return out


def row(ref_value, r):
    return ref_value[r * SUBS : (r + 1) * SUBS]


def pair_up(a, b):
    return jnp.concatenate([a, b], 0)


def split(x):
    high = x.astype(BF16)
    low = (x - high.astype(F32)).astype(BF16)
    return high, low


def root(x):
    return x * lax.rsqrt(jnp.maximum(x, TINY))


def dot(a, b):
    return jnp.dot(a, b, preferred_element_type=F32)


def prepare_own(own_ref, own32_ref):
    for i in range(2):
        for q in range(EXT // 2):
            at = pl.ds(q * 16, 16)
            re = own_ref[i, 0, at, :].astype(F32)
            im = own_ref[i, 1, at, :].astype(F32)
            own32_ref[i, 0, at, :] = re
            own32_ref[i, 1, at, :] = im
            own32_ref[i, 2, at, :] = re * re + im * im


def compute_pair(
    first, start, end, own32, other, tables, put_coherence, put_filtered, box_in, ml, mid, spec_in, mags, mag_in
):
    box_t, forward_t, inverse_t, near_t, same_t = tables
    sub = lax.broadcasted_iota(jnp.int32, (SUBS, LANES), 0)
    lane = lax.broadcasted_iota(jnp.int32, (SUBS, LANES), 1)
    low_half = lane < LANES // 2
    inner = jnp.where(low_half, jnp.where(sub > 0, 1.0, 0.0), jnp.where(sub < SUBS - 1, 1.0, 0.0))
    masks = []
    for r in range(EXT):
        here = first + (r - HALO)
        masks.append(jnp.where((here >= start) & (here < end), 1.0, 0.0).astype(F32))

    kept = [[], [], [], []]

    def add_products(q):
        at = pl.ds(q * 16, 16)
        c_re2 = other(0, at).astype(F32)
        c_im2 = other(1, at).astype(F32)
        for half in range(2):
            r = 2 * q + half
            m = masks[r]
            one = pl.ds(r * SUBS, SUBS)
            a_re = own32(0, one) * m
            a_im = own32(1, one) * m
            c_re, c_im = row(c_re2, half), row(c_im2, half)
            kept[0].append(a_re * c_re + a_im * c_im)
            kept[1].append(a_im * c_re - a_re * c_im)
            kept[2].append(own32(2, one) * m)
            kept[3].append((c_re * c_re + c_im * c_im) * m)

    add_products(0)
    add_products(1)
    two = [[kept[f][n] + kept[f][n + 1] for n in range(3)] for f in range(4)]
    for g in range(ROWS // SUBS):
        for q in range(4):
            add_products(2 + g * 4 + q)
            for f in range(4):
                sums = []
                for half in range(2):
                    r = g * 8 + q * 2 + half
                    two[f].append(kept[f][r + 3] + kept[f][r + 4])
                    sums.append(kept[f][r] + (two[f][r + 1] + two[f][r + 3]))
                high, low = split(pair_up(*sums))
                at = pl.ds(f * 64 + q * 16, 16)
                box_in[g % 2, at, 0:LANES] = high
                box_in[g % 2, at, LANES : 2 * LANES] = low
        y = dot(box_in[g % 2], box_t[...])
        for n in range(8):
            r = g * 8 + n
            ml_f = []
            for f in range(4):
                base = (f * 8 + n) * SUBS
                own_part = y[base : base + SUBS, 0:LANES]
                side = y[base : base + SUBS, LANES : 2 * LANES]
                side = jnp.where(low_half, pltpu.roll(side, 1, 0), pltpu.roll(side, SUBS - 1, 0))
                ml_f.append(own_part + side * inner)
            re, im, p1, p2 = ml_f
            ml[0, pl.ds(r * SUBS, SUBS), :] = re
            ml[1, pl.ds(r * SUBS, SUBS), :] = im
            size = root(re * re + im * im)
            down = lax.rsqrt(p1 * p2 + 1e-6 * BOX_RATIO * BOX_RATIO)
            put_coherence(r, size * (down * masks[r + HALO]))

    for b in range(8):
        x = [
            (ml[0, pl.ds((b + 8 * a) * SUBS, SUBS), :], ml[1, pl.ds((b + 8 * a) * SUBS, SUBS), :])
            for a in range(4)
        ]
        x = dft4(x, -1)
        for k1 in range(4):
            v = cmul(x[k1], -2 * math.pi * b * k1 / 32)
            mid[0, pl.ds((k1 * 8 + b) * SUBS, SUBS), :] = v[0]
            mid[1, pl.ds((k1 * 8 + b) * SUBS, SUBS), :] = v[1]

    def put_split(place, parts):
        for c in range(2):
            high, low = split(pair_up(parts[0][c], parts[1][c]))
            at = pl.ds(place * SUBS, 16)
            spec_in[at, c * LANES : (c + 1) * LANES] = high
            spec_in[at, (2 + c) * LANES : (3 + c) * LANES] = low

    for k1 in range(4):
        x = [
            (mid[0, pl.ds((k1 * 8 + b) * SUBS, SUBS), :], mid[1, pl.ds((k1 * 8 + b) * SUBS, SUBS), :])
            for b in range(8)
        ]
        x = dft8(x, -1)
        for k2 in range(0, 8, 2):
            put_split(k1 * 8 + k2, x[k2 : k2 + 2])

    both = spec_in[...]
    s = dot(jnp.concatenate([both, both[:, 0 : 2 * LANES]], 1), forward_t[...])
    for p in range(ROWS):
        at = pl.ds(p * SUBS, SUBS)
        re, im = row(s, p)[:, 0:LANES], row(s, p)[:, LANES:]
        mid[0, at, :] = re
        mid[1, at, :] = im
        mags[at, :] = root(re * re + im * im)

    def place(k):
        k = k % PATCH
        return (k % 4) * 8 + k // 4

    total = None
    for p in range(0, ROWS, 2):
        sums = []
        for k in (p // 8 + 4 * (p % 8), p // 8 + 4 * (p % 8 + 1)):
            sums.append(
                mags[pl.ds(place(k - 1) * SUBS, SUBS), :]
                + mags[pl.ds(place(k) * SUBS, SUBS), :]
                + mags[pl.ds(place(k + 1) * SUBS, SUBS), :]
            )
            total = sums[-1] if total is None else total + sums[-1]
        high, low = split(pair_up(*sums))
        mag_in[pl.ds(p * SUBS, 16), 0:LANES] = high
        mag_in[pl.ds(p * SUBS, 16), LANES:] = low
    high, low = split(pair_up(total, total))
    tile_sum = dot(jnp.concatenate([high, low], 1), same_t[...])[0:SUBS]
    inv = (1.0 / 9.0) / (tile_sum * (1.0 / (3 * PATCH * PATCH)) + 1e-6 / (PATCH * PATCH))
    smooth = dot(mag_in[...], near_t[...])
    for p in range(0, ROWS, 2):
        parts = []
        for n in (p, p + 1):
            w = root(row(smooth, n) * inv)
            at = pl.ds(n * SUBS, SUBS)
            parts.append((mid[0, at, :] * w, mid[1, at, :] * w))
        put_split(p, parts)

    both = spec_in[...]
    s = dot(jnp.concatenate([both, both[:, 0 : 2 * LANES]], 1), inverse_t[...])
    for k1 in range(4):
        x = [
            (row(s, k1 * 8 + k2)[:, 0:LANES], row(s, k1 * 8 + k2)[:, LANES:])
            for k2 in range(8)
        ]
        x = dft8(x, 1)
        for b in range(8):
            v = cmul(x[b], 2 * math.pi * b * k1 / 32)
            at = pl.ds((k1 * 8 + b) * SUBS, SUBS)
            mid[0, at, :] = v[0]
            mid[1, at, :] = v[1]
    for b in range(8):
        x = [
            (mid[0, pl.ds((k1 * 8 + b) * SUBS, SUBS), :], mid[1, pl.ds((k1 * 8 + b) * SUBS, SUBS), :])
            for k1 in range(4)
        ]
        x = dft4(x, 1)
        for a in range(4):
            r = b + 8 * a
            put_filtered(0, r, x[a][0] * masks[r + HALO])
            put_filtered(1, r, x[a][1] * masks[r + HALO])


def compute_kernel(
    partner, valid, own, other, box_t, forward_t, inverse_t, near_t, same_t, coherence, filtered,
    own32, box_in, ml, mid, spec_in, mags, mag_in,
):
    rnd = pl.program_id(0)
    first = lax.axis_index("strip") * ROWS
    tables = (box_t, forward_t, inverse_t, near_t, same_t)

    @pl.when(rnd == 0)
    def _():
        prepare_own(own, own32)

    for i in range(2):
        which = partner[rnd, 0, i]

        def put_coherence(r, value, i=i):
            coherence[0, i, r // 8, pl.ds(r % 8, SUBS, stride=8), :] = value

        def put_filtered(c, r, value, i=i):
            filtered[0, i, c, r // 8, pl.ds(r % 8, SUBS, stride=8), :] = value

        compute_pair(
            first,
            valid[rnd, i, 0],
            valid[rnd, i, 1],
            lambda c, at, i=i: own32[i, c, at, :],
            lambda c, at, which=which: other[rnd, which, c, at, :],
            tables,
            put_coherence,
            put_filtered,
            box_in.at[i],
            ml.at[i],
            mid.at[i],
            spec_in.at[i],
            mags.at[i],
            mag_in.at[i],
        )


def compute(partner, valid, own, other):
    tables = [jnp.asarray(t) for t in make_tables()]
    vmem = pl.BlockSpec(memory_space=pltpu.VMEM)
    smem = pl.BlockSpec(memory_space=pltpu.SMEM)
    rounds = other.shape[0]
    return pl.pallas_call(
        compute_kernel,
        grid=(rounds,),
        out_shape=(
            jax.ShapeDtypeStruct((rounds, 2, 4, 64, LANES), F32),
            jax.ShapeDtypeStruct((rounds, 2, 2, 4, 64, LANES), F32),
        ),
        in_specs=[smem, smem] + [vmem] * 7,
        out_specs=(
            pl.BlockSpec((1, 2, 4, 64, LANES), lambda r: (r, 0, 0, 0, 0)),
            pl.BlockSpec((1, 2, 2, 4, 64, LANES), lambda r: (r, 0, 0, 0, 0, 0)),
        ),
        scratch_shapes=[
            pltpu.VMEM((2, 3, FULL, LANES), F32),
            pltpu.VMEM((2, 2, 256, 2 * LANES), BF16),
            pltpu.VMEM((2, 2, BODY, LANES), F32),
            pltpu.VMEM((2, 2, BODY, LANES), F32),
            pltpu.VMEM((2, BODY, 4 * LANES), BF16),
            pltpu.VMEM((2, BODY, LANES), F32),
            pltpu.VMEM((2, BODY, 2 * LANES), BF16),
        ],
        compiler_params=pltpu.CompilerParams(vmem_limit_bytes=48 * 1024 * 1024),
    )(partner, valid, own, other, *tables)


def exchange_kernel(slc, own, other, lines, halo_send, halo_recv, main_send, main_recv, edge_send, edge_recv, fwd_send, fwd_recv, fwde_send, fwde_recv):
    date = lax.axis_index("date")
    strip = lax.axis_index("strip")
    n_strip = lax.axis_size("strip")
    above = (date, lax.rem(strip + n_strip - 1, n_strip))
    below = (date, lax.rem(strip + 1, n_strip))

    def xor(bits):
        target = date
        for bit in range(4):
            if bits >> bit & 1:
                size = 1 << bit
                target = target + size - 2 * size * lax.rem(lax.div(date, size), 2)
        return (target, strip)

    partners = {0: xor(1), 1: xor(2), 3: xor(8)}
    onward = xor(6)

    barrier = pltpu.get_barrier_semaphore()
    greeted = [above, below, partners[0], partners[1], partners[3], onward]
    for device in greeted:
        pl.semaphore_signal(barrier, inc=1, device_id=device, device_id_type=MESH)

    for i in range(2):
        for c in range(2):
            for g in range(4):
                for j in range(8):
                    lines[i * 2 + c, g, pl.ds(j * 8, 8), :] = slc[
                        i, c, pl.ds(g * 8, 8), pl.ds(j * LANES, LANES)
                    ].astype(F32)
            for g in range(4):
                for s in range(0, 8, 2):
                    pair = jnp.concatenate(
                        [
                            lines[i * 2 + c, g, pl.ds(s, 8, stride=8), :],
                            lines[i * 2 + c, g, pl.ds(s + 1, 8, stride=8), :],
                        ],
                        0,
                    )
                    own[i, c, pl.ds(EDGE + (g * 8 + s) * SUBS, 16), :] = pair.astype(BF16)

    pl.semaphore_wait(barrier, len(greeted))

    top, bottom = pl.ds(0, EDGE), pl.ds(FULL - EDGE, EDGE)
    first_rows, last_rows = pl.ds(EDGE, EDGE), pl.ds(FULL - 2 * EDGE, EDGE)
    body = pl.ds(EDGE, BODY)

    def send(src, dst, send_sem, recv_sem, device):
        copy = pltpu.make_async_remote_copy(
            src_ref=src, dst_ref=dst, send_sem=send_sem, recv_sem=recv_sem, device_id=device, device_id_type=MESH
        )
        copy.start()
        return copy

    to_above = send(own.at[:, :, first_rows], own.at[:, :, bottom], halo_send.at[0], halo_recv.at[0], above)
    to_below = send(own.at[:, :, last_rows], own.at[:, :, top], halo_send.at[1], halo_recv.at[1], below)

    mains = {}
    for i in range(2):
        for c in range(2):
            for n, r in enumerate((1, 3, 0)):
                mains[r, i, c] = send(
                    own.at[i, c, body],
                    other.at[r, i, c, body],
                    main_send.at[n, i, c],
                    main_recv.at[n, i, c],
                    partners[r],
                )
    to_above.wait_recv()
    to_below.wait_recv()
    edges = {}
    for n, r in enumerate((1, 3, 0)):
        for side, at in enumerate((top, bottom)):
            edges[r, side] = send(
                own.at[:, :, at], other.at[r, :, :, at], edge_send.at[n, side], edge_recv.at[n, side], partners[r]
            )
    forwards = []
    for i in range(2):
        for c in range(2):
            mains[1, i, c].wait_recv()
            forwards.append(
                send(
                    other.at[1, i, c, body], other.at[2, i, c, body], fwd_send.at[i, c], fwd_recv.at[i, c], onward
                )
            )
    for side, at in enumerate((top, bottom)):
        edges[1, side].wait_recv()
        forwards.append(
            send(other.at[1, :, :, at], other.at[2, :, :, at], fwde_send.at[side], fwde_recv.at[side], onward)
        )
    to_above.wait_send()
    to_below.wait_send()
    for (r, _, _), copy in mains.items():
        copy.wait_send()
        if r != 1:
            copy.wait_recv()
    for (r, _), copy in edges.items():
        copy.wait_send()
        if r != 1:
            copy.wait_recv()
    for copy in forwards:
        copy.wait()


def exchange(slc):
    vmem = pl.BlockSpec(memory_space=pltpu.VMEM)
    dma = pltpu.SemaphoreType.DMA
    return pl.pallas_call(
        exchange_kernel,
        out_shape=(
            jax.ShapeDtypeStruct((2, 2, FULL, LANES), BF16),
            jax.ShapeDtypeStruct((4, 2, 2, FULL, LANES), BF16),
        ),
        in_specs=[vmem],
        out_specs=(vmem, vmem),
        scratch_shapes=[
            pltpu.VMEM((4, 4, 64, LANES), F32),
            dma((2,)),
            dma((2,)),
            dma((3, 2, 2)),
            dma((3, 2, 2)),
            dma((3, 2)),
            dma((3, 2)),
            dma((2, 2)),
            dma((2, 2)),
            dma((2,)),
            dma((2,)),
        ],
        compiler_params=pltpu.CompilerParams(
            collective_id=0, has_side_effects=True, vmem_limit_bytes=32 * 1024 * 1024
        ),
    )(slc)


def untile(array):
    lead = array.shape[:-3]
    array = array.reshape(lead + (4, 8, 8, LANES))
    n = len(lead)
    array = array.transpose(tuple(range(n)) + (n, n + 2, n + 1, n + 3))
    return array.reshape(lead + (ROWS, 8 * LANES))


def shards(slc, partner, valid):
    own, other = exchange(slc)
    coherence, filtered = compute(partner, valid, own, other)
    return untile(coherence), untile(filtered)


def solution(mesh):
    in_specs = (P("date", None, "strip", None), P(None, "date", None), P(None, "date", None))
    out_specs = (P(None, "date", "strip", None), P(None, "date", None, "strip", None))
    return jax.shard_map(shards, mesh=mesh, in_specs=in_specs, out_specs=out_specs, check_vma=False)
```

profile of v0, /device:TPU:1, one launch (start us, length us, event | category | flops | bytes accessed | tf_op | source)
XLA Modules:
  0.0 41.9 jit_solution(6654604267195422729)
XLA Ops:
  0.6 0.8 %copy.10.partner = s32[4,1,2]{2,1,0:T(1,128)S(1)} copy(s32[4,1,2]{0,2,1:T(2,128)} %param.9) | data formatting | bytes 64 | tf_op args[1]
  1.4 0.8 %copy.11.valid = s32[4,2,2]{2,1,0:T(2,128)S(1)} copy(s32[4,2,2]{0,2,1:T(2,128)} %param.10) | data formatting | bytes 128 | tf_op args[2]
  2.2 0.0 copy-start.2
  2.2 0.9 %copy-done.2 = bf16[2,2,32,1024]{3,2,1,0:T(8,128)(2,1)S(1)} copy-done((bf16[2,2,32,1024]{3,2,1,0:T(8,128)(2,1)S(1)}, bf16[2,2,32,1024]{3,2,1,0:T(8,128)(2,1)}, u32[]{:S(2)}) %copy-start.2) | copy-done | bytes 262168
  3.1 22.7 %shard_map.95 = (bf16[2,2,288,128]{3,2,1,0:T(8,128)(2,1)S(1)}, bf16[4,2,2,288,128]{4,3,2,1,0:T(8,128)(2,1)S(1)}) custom-call(bf16[2,2,32,1024]{3,2,1,0:T(8,128)(2,1)S(1)} %copy-done.2), custom_call_target="tpu_custom_call" | custom-call | tf_op jit(solution)/shard_map/pallas_call | solution.py:492
  25.8 0.0 copy-start
  25.8 1.0 %copy-done = bf16[768,256]{1,0:T(8,128)(2,1)S(1)} copy-done((bf16[768,256]{1,0:T(8,128)(2,1)S(1)}, bf16[768,256]{1,0:T(8,128)(2,1)}, u32[]{:S(2)}) %copy-start) | copy-done | bytes 393240
  26.8 0.0 copy-start.1
  26.8 1.0 %copy-done.1 = bf16[768,256]{1,0:T(8,128)(2,1)S(1)} copy-done((bf16[768,256]{1,0:T(8,128)(2,1)S(1)}, bf16[768,256]{1,0:T(8,128)(2,1)}, u32[]{:S(2)}) %copy-start.1) | copy-done | bytes 393240
  27.8 0.0 copy-start.3
  27.8 0.9 %copy-done.3 = bf16[256,256]{1,0:T(8,128)(2,1)S(1)} copy-done((bf16[256,256]{1,0:T(8,128)(2,1)S(1)}, bf16[256,256]{1,0:T(8,128)(2,1)}, u32[]{:S(2)}) %copy-start.3) | copy-done | bytes 131096
  28.7 0.0 copy-start.4
  28.7 0.8 %copy-done.4 = bf16[256,128]{1,0:T(8,128)(2,1)S(1)} copy-done((bf16[256,128]{1,0:T(8,128)(2,1)S(1)}, bf16[256,128]{1,0:T(8,128)(2,1)}, u32[]{:S(2)}) %copy-start.4) | copy-done | bytes 65560
  29.5 0.0 copy-start.5
  29.5 0.8 %copy-done.5 = bf16[256,128]{1,0:T(8,128)(2,1)S(1)} copy-done((bf16[256,128]{1,0:T(8,128)(2,1)S(1)}, bf16[256,128]{1,0:T(8,128)(2,1)}, u32[]{:S(2)}) %copy-start.5) | copy-done | bytes 65560
  30.4 11.6 %shard_map.96 = (f32[4,2,4,64,128]{4,3,2,1,0:T(8,128)}, f32[4,2,2,4,64,128]{5,4,3,2,1,0:T(8,128)}) custom-call(s32[4,1,2]{2,1,0:T(1,128)S(1)} %copy.10.partner, s32[4,2,2]{2,1,0:T(2,128)S(1)} %copy.11.valid, bf16[2,2,288,128]{3,2,1,0:T(8,128)(2,1)S(1)} %get-tuple-element.6.own, bf16[4,2,2,288,128]{4,3,2,1,0:T(8,128)(2,1)S(1)} %get-tuple-element.7.other, ...), custom_call_target="tpu_custom_call" | custom-call | tf_op jit(solution)/shard_map/pallas_call | solution.py:360
Async XLA Ops:
  2.2 0.9 %copy-start.2 = (bf16[2,2,32,1024]{3,2,1,0:T(8,128)(2,1)S(1)}, bf16[2,2,32,1024]{3,2,1,0:T(8,128)(2,1)}, u32[]{:S(2)}) copy-start(bf16[2,2,32,1024]{3,2,1,0:T(8,128)(2,1)} %slc.1) | copy-start | bytes 786436
  25.8 1.0 %copy-start = (bf16[768,256]{1,0:T(8,128)(2,1)S(1)}, bf16[768,256]{1,0:T(8,128)(2,1)}, u32[]{:S(2)}) copy-start(bf16[768,256]{1,0:T(8,128)(2,1)} %constant.12.clone.inverse_t) | copy-start | bytes 1179652
  26.8 1.0 %copy-start.1 = (bf16[768,256]{1,0:T(8,128)(2,1)S(1)}, bf16[768,256]{1,0:T(8,128)(2,1)}, u32[]{:S(2)}) copy-start(bf16[768,256]{1,0:T(8,128)(2,1)} %constant.11.clone.forward_t) | copy-start | bytes 1179652
  27.8 0.9 %copy-start.3 = (bf16[256,256]{1,0:T(8,128)(2,1)S(1)}, bf16[256,256]{1,0:T(8,128)(2,1)}, u32[]{:S(2)}) copy-start(bf16[256,256]{1,0:T(8,128)(2,1)} %constant.10.clone.box_t) | copy-start | bytes 393220
  28.7 0.8 %copy-start.4 = (bf16[256,128]{1,0:T(8,128)(2,1)S(1)}, bf16[256,128]{1,0:T(8,128)(2,1)}, u32[]{:S(2)}) copy-start(bf16[256,128]{1,0:T(8,128)(2,1)} %constant.14.clone.same_t) | copy-start | bytes 196612
  29.5 0.8 %copy-start.5 = (bf16[256,128]{1,0:T(8,128)(2,1)S(1)}, bf16[256,128]{1,0:T(8,128)(2,1)}, u32[]{:S(2)}) copy-start(bf16[256,128]{1,0:T(8,128)(2,1)} %constant.13.clone.near_t) | copy-start | bytes 196612
where the time goes:
time: 42.3 us; the launch traced here: 41.9 us
  Pallas kernels  34.2 us (81%)
  local copies, waits for them, and re-layouts  7.06 us (17%)
  between operations  0.65 us (2%)
    pallas_call x1, Pallas kernels, exchange(): pl.pallas_call(exchange_kernel, out_shape=(jax.ShapeDtypeStruct((2, 2, FU...  22.7 us
    pallas_call x1, Pallas kernels, compute(): pl.pallas_call(compute_kernel, grid=(rounds,), out_shape=(jax.ShapeDtypeS...  11.6 us
    unnamed x14, local copies, waits for them, and re-layouts  7.06 us

commit v1 on v0

--- a/solution.py
+++ b/solution.py
@@ -146,17 +146,6 @@
 
 def dot(a, b):
     return jnp.dot(a, b, preferred_element_type=F32)
-
-
-def prepare_own(own_ref, own32_ref):
-    for i in range(2):
-        for q in range(EXT // 2):
-            at = pl.ds(q * 16, 16)
-            re = own_ref[i, 0, at, :].astype(F32)
-            im = own_ref[i, 1, at, :].astype(F32)
-            own32_ref[i, 0, at, :] = re
-            own32_ref[i, 1, at, :] = im
-            own32_ref[i, 2, at, :] = re * re + im * im
 
 
 def compute_pair(
@@ -313,81 +302,50 @@
             put_filtered(1, r, x[a][1] * masks[r + HALO])
 
 
-def compute_kernel(
-    partner, valid, own, other, box_t, forward_t, inverse_t, near_t, same_t, coherence, filtered,
-    own32, box_in, ml, mid, spec_in, mags, mag_in,
-):
-    rnd = pl.program_id(0)
-    first = lax.axis_index("strip") * ROWS
-    tables = (box_t, forward_t, inverse_t, near_t, same_t)
-
-    @pl.when(rnd == 0)
-    def _():
-        prepare_own(own, own32)
-
+def compute_round(rnd, first, partner, valid, own32, other, tables, coherence, filtered, scratch):
     for i in range(2):
-        which = partner[rnd, 0, i]
+        which = partner[0, i, rnd]
 
         def put_coherence(r, value, i=i):
-            coherence[0, i, r // 8, pl.ds(r % 8, SUBS, stride=8), :] = value
+            coherence[i, r // 8, pl.ds(r % 8, SUBS, stride=8), :] = value
 
         def put_filtered(c, r, value, i=i):
-            filtered[0, i, c, r // 8, pl.ds(r % 8, SUBS, stride=8), :] = value
+            filtered[i, c, r // 8, pl.ds(r % 8, SUBS, stride=8), :] = value
 
         compute_pair(
             first,
-            valid[rnd, i, 0],
-            valid[rnd, i, 1],
+            valid[i, 0, rnd],
+            valid[i, 1, rnd],
             lambda c, at, i=i: own32[i, c, at, :],
-            lambda c, at, which=which: other[rnd, which, c, at, :],
+            lambda c, at, which=which: jnp.where(which == 0, other[rnd, 0, c, at, :], other[rnd, 1, c, at, :]),
             tables,
             put_coherence,
             put_filtered,
-            box_in.at[i],
-            ml.at[i],
-            mid.at[i],
-            spec_in.at[i],
-            mags.at[i],
-            mag_in.at[i],
+            *[ref.at[i] for ref in scratch],
         )
 
 
-def compute(partner, valid, own, other):
-    tables = [jnp.asarray(t) for t in make_tables()]
-    vmem = pl.BlockSpec(memory_space=pltpu.VMEM)
-    smem = pl.BlockSpec(memory_space=pltpu.SMEM)
-    rounds = other.shape[0]
-    return pl.pallas_call(
-        compute_kernel,
-        grid=(rounds,),
-        out_shape=(
-            jax.ShapeDtypeStruct((rounds, 2, 4, 64, LANES), F32),
-            jax.ShapeDtypeStruct((rounds, 2, 2, 4, 64, LANES), F32),
-        ),
-        in_specs=[smem, smem] + [vmem] * 7,
-        out_specs=(
-            pl.BlockSpec((1, 2, 4, 64, LANES), lambda r: (r, 0, 0, 0, 0)),
-            pl.BlockSpec((1, 2, 2, 4, 64, LANES), lambda r: (r, 0, 0, 0, 0, 0)),
-        ),
-        scratch_shapes=[
-            pltpu.VMEM((2, 3, FULL, LANES), F32),
-            pltpu.VMEM((2, 2, 256, 2 * LANES), BF16),
-            pltpu.VMEM((2, 2, BODY, LANES), F32),
-            pltpu.VMEM((2, 2, BODY, LANES), F32),
-            pltpu.VMEM((2, BODY, 4 * LANES), BF16),
-            pltpu.VMEM((2, BODY, LANES), F32),
-            pltpu.VMEM((2, BODY, 2 * LANES), BF16),
-        ],
-        compiler_params=pltpu.CompilerParams(vmem_limit_bytes=48 * 1024 * 1024),
-    )(partner, valid, own, other, *tables)
-
-
-def exchange_kernel(slc, own, other, lines, halo_send, halo_recv, main_send, main_recv, edge_send, edge_recv, fwd_send, fwd_recv, fwde_send, fwde_recv):
+def work_shapes():
+    return [
+        pltpu.VMEM((2, 2, 256, 2 * LANES), BF16),
+        pltpu.VMEM((2, 2, BODY, LANES), F32),
+        pltpu.VMEM((2, 2, BODY, LANES), F32),
+        pltpu.VMEM((2, BODY, 4 * LANES), BF16),
+        pltpu.VMEM((2, BODY, LANES), F32),
+        pltpu.VMEM((2, BODY, 2 * LANES), BF16),
+    ]
+
+
+def exchange_kernel(
+    partner_hbm, valid_hbm, slc_hbm, box_h, forward_h, inverse_h, near_h, same_h,
+    coherence_hbm, filtered_hbm,
+    own32, other, coherence, filtered, box_t, forward_t, inverse_t, near_t, same_t,
+    slc, own, lines, partner, valid, load_sem, out_sem,
+    halo_send, halo_recv, main_send, main_recv, edge_send, edge_recv, fwd_send, fwd_recv, *work,
+):
     date = lax.axis_index("date")
     strip = lax.axis_index("strip")
     n_strip = lax.axis_size("strip")
-    above = (date, lax.rem(strip + n_strip - 1, n_strip))
-    below = (date, lax.rem(strip + 1, n_strip))
 
     def xor(bits):
         target = date
@@ -395,16 +353,47 @@
             if bits >> bit & 1:
                 size = 1 << bit
                 target = target + size - 2 * size * lax.rem(lax.div(date, size), 2)
-        return (target, strip)
-
-    partners = {0: xor(1), 1: xor(2), 3: xor(8)}
-    onward = xor(6)
+        return target
+
+    mate, onward = xor(1), xor(6)
+    partners = {0: mate, 1: xor(2), 2: xor(4), 3: xor(8)}
+    has_above, has_below = strip > 0, strip < n_strip - 1
+
+    loads = []
+    for n, (src, dst) in enumerate(
+        [
+            (slc_hbm, slc),
+            (partner_hbm, partner),
+            (valid_hbm, valid),
+            (box_h, box_t),
+            (forward_h, forward_t),
+            (near_h, near_t),
+            (same_h, same_t),
+            (inverse_h, inverse_t),
+        ]
+    ):
+        loads.append(pltpu.make_async_copy(src, dst, load_sem.at[n]))
+        loads[-1].start()
 
     barrier = pltpu.get_barrier_semaphore()
-    greeted = [above, below, partners[0], partners[1], partners[3], onward]
-    for device in greeted:
+
+    def greet(device):
         pl.semaphore_signal(barrier, inc=1, device_id=device, device_id_type=MESH)
 
+    @pl.when(has_above)
+    def _():
+        greet((date, strip - 1))
+        greet((mate, strip - 1))
+
+    @pl.when(has_below)
+    def _():
+        greet((date, strip + 1))
+        greet((mate, strip + 1))
+
+    for device in (*partners.values(), onward):
+        greet((device, strip))
+
+    loads[0].wait()
     for i in range(2):
         for c in range(2):
             for g in range(4):
@@ -423,97 +412,233 @@
                     )
                     own[i, c, pl.ds(EDGE + (g * 8 + s) * SUBS, 16), :] = pair.astype(BF16)
 
-    pl.semaphore_wait(barrier, len(greeted))
-
     top, bottom = pl.ds(0, EDGE), pl.ds(FULL - EDGE, EDGE)
     first_rows, last_rows = pl.ds(EDGE, EDGE), pl.ds(FULL - 2 * EDGE, EDGE)
     body = pl.ds(EDGE, BODY)
-
-    def send(src, dst, send_sem, recv_sem, device):
-        copy = pltpu.make_async_remote_copy(
+    blank = jnp.zeros((EDGE, LANES), BF16)
+
+    @pl.when(jnp.logical_not(has_above))
+    def _():
+        for i in range(2):
+            for c in range(2):
+                own[i, c, top, :] = blank
+                other[0, i, c, top, :] = blank
+
+    @pl.when(jnp.logical_not(has_below))
+    def _():
+        for i in range(2):
+            for c in range(2):
+                own[i, c, bottom, :] = blank
+                other[0, i, c, bottom, :] = blank
+
+    def remote(src, dst, send_sem, recv_sem, device):
+        return pltpu.make_async_remote_copy(
             src_ref=src, dst_ref=dst, send_sem=send_sem, recv_sem=recv_sem, device_id=device, device_id_type=MESH
         )
-        copy.start()
-        return copy
-
-    to_above = send(own.at[:, :, first_rows], own.at[:, :, bottom], halo_send.at[0], halo_recv.at[0], above)
-    to_below = send(own.at[:, :, last_rows], own.at[:, :, top], halo_send.at[1], halo_recv.at[1], below)
+
+    up = [
+        remote(own.at[:, :, first_rows], own.at[:, :, bottom], halo_send.at[0], halo_recv.at[0], (date, strip - 1)),
+        remote(
+            own.at[:, :, first_rows], other.at[0, :, :, bottom], halo_send.at[2], halo_recv.at[2], (mate, strip - 1)
+        ),
+    ]
+    down = [
+        remote(own.at[:, :, last_rows], own.at[:, :, top], halo_send.at[1], halo_recv.at[1], (date, strip + 1)),
+        remote(own.at[:, :, last_rows], other.at[0, :, :, top], halo_send.at[3], halo_recv.at[3], (mate, strip + 1)),
+    ]
+    inside = has_above & has_below
+
+    @pl.when(inside)
+    def _():
+        pl.semaphore_wait(barrier, 9)
+
+    @pl.when(jnp.logical_not(inside))
+    def _():
+        pl.semaphore_wait(barrier, 7)
+
+    @pl.when(has_above)
+    def _():
+        for copy in up:
+            copy.start()
+
+    @pl.when(has_below)
+    def _():
+        for copy in down:
+            copy.start()
 
     mains = {}
     for i in range(2):
         for c in range(2):
             for n, r in enumerate((1, 3, 0)):
-                mains[r, i, c] = send(
+                mains[r, i, c] = remote(
                     own.at[i, c, body],
                     other.at[r, i, c, body],
                     main_send.at[n, i, c],
                     main_recv.at[n, i, c],
-                    partners[r],
+                    (partners[r], strip),
                 )
-    to_above.wait_recv()
-    to_below.wait_recv()
+                mains[r, i, c].start()
+
+    def widen(i, q):
+        at = pl.ds(q * 16, 16)
+        re = own[i, 0, at, :].astype(F32)
+        im = own[i, 1, at, :].astype(F32)
+        own32[i, 0, at, :] = re
+        own32[i, 1, at, :] = im
+        own32[i, 2, at, :] = re * re + im * im
+
+    for i in range(2):
+        for q in range(1, EXT // 2 - 1):
+            widen(i, q)
+
+    @pl.when(has_below)
+    def _():
+        up[0].wait_recv()
+
+    @pl.when(has_above)
+    def _():
+        down[0].wait_recv()
+
     edges = {}
-    for n, r in enumerate((1, 3, 0)):
+    for n, r in enumerate((1, 2, 3)):
         for side, at in enumerate((top, bottom)):
-            edges[r, side] = send(
-                own.at[:, :, at], other.at[r, :, :, at], edge_send.at[n, side], edge_recv.at[n, side], partners[r]
+            edges[r, side] = remote(
+                own.at[:, :, at],
+                other.at[r, :, :, at],
+                edge_send.at[n, side],
+                edge_recv.at[n, side],
+                (partners[r], strip),
             )
+            edges[r, side].start()
+    for i in range(2):
+        for q in (0, EXT // 2 - 1):
+            widen(i, q)
+
     forwards = []
     for i in range(2):
         for c in range(2):
             mains[1, i, c].wait_recv()
             forwards.append(
-                send(
-                    other.at[1, i, c, body], other.at[2, i, c, body], fwd_send.at[i, c], fwd_recv.at[i, c], onward
+                remote(
+                    other.at[1, i, c, body],
+                    other.at[2, i, c, body],
+                    fwd_send.at[i, c],
+                    fwd_recv.at[i, c],
+                    (onward, strip),
                 )
             )
-    for side, at in enumerate((top, bottom)):
-        edges[1, side].wait_recv()
-        forwards.append(
-            send(other.at[1, :, :, at], other.at[2, :, :, at], fwde_send.at[side], fwde_recv.at[side], onward)
+            forwards[-1].start()
+    for i in range(2):
+        for c in range(2):
+            mains[0, i, c].wait_recv()
+
+    @pl.when(has_below)
+    def _():
+        up[1].wait_recv()
+
+    @pl.when(has_above)
+    def _():
+        down[1].wait_recv()
+
+    for copy in loads[1:]:
+        copy.wait()
+    tables = (box_t, forward_t, inverse_t, near_t, same_t)
+
+    def outputs(rnd):
+        return [
+            pltpu.make_async_copy(coherence.at[rnd], coherence_hbm.at[rnd], out_sem.at[rnd, 0]),
+            pltpu.make_async_copy(filtered.at[rnd], filtered_hbm.at[rnd], out_sem.at[rnd, 1]),
+        ]
+
+    def one_round(rnd, carry):
+        @pl.when(rnd == 1)
+        def _():
+            edges[1, 0].wait_recv()
+            edges[1, 1].wait_recv()
+
+        @pl.when(rnd == 2)
+        def _():
+            for copy in forwards:
+                copy.wait_recv()
+            edges[2, 0].wait_recv()
+            edges[2, 1].wait_recv()
+
+        @pl.when(rnd == 3)
+        def _():
+            for i in range(2):
+                for c in range(2):
+                    mains[3, i, c].wait_recv()
+            edges[3, 0].wait_recv()
+            edges[3, 1].wait_recv()
+
+        compute_round(
+            rnd, strip * ROWS, partner, valid, own32, other, tables, coherence.at[rnd], filtered.at[rnd], work
         )
-    to_above.wait_send()
-    to_below.wait_send()
-    for (r, _, _), copy in mains.items():
+        for copy in outputs(rnd):
+            copy.start()
+        return carry
+
+    lax.fori_loop(0, 4, one_round, 0)
+
+    @pl.when(has_above)
+    def _():
+        for copy in up:
+            copy.wait_send()
+
+    @pl.when(has_below)
+    def _():
+        for copy in down:
+            copy.wait_send()
+
+    for copy in (*mains.values(), *edges.values(), *forwards):
         copy.wait_send()
-        if r != 1:
-            copy.wait_recv()
-    for (r, _), copy in edges.items():
-        copy.wait_send()
-        if r != 1:
-            copy.wait_recv()
-    for copy in forwards:
-        copy.wait()
-
-
-def exchange(slc):
-    vmem = pl.BlockSpec(memory_space=pltpu.VMEM)
+    for rnd in range(4):
+        for copy in outputs(rnd):
+            copy.wait()
+
+
+def exchange(partner, valid, slc):
+    tables = [jnp.asarray(t) for t in make_tables()]
+    hbm = pl.BlockSpec(memory_space=pltpu.HBM)
     dma = pltpu.SemaphoreType.DMA
     return pl.pallas_call(
         exchange_kernel,
         out_shape=(
-            jax.ShapeDtypeStruct((2, 2, FULL, LANES), BF16),
-            jax.ShapeDtypeStruct((4, 2, 2, FULL, LANES), BF16),
+            jax.ShapeDtypeStruct((4, 2, 4, 64, LANES), F32),
+            jax.ShapeDtypeStruct((4, 2, 2, 4, 64, LANES), F32),
         ),
-        in_specs=[vmem],
-        out_specs=(vmem, vmem),
+        in_specs=[hbm] * 8,
+        out_specs=(hbm, hbm),
         scratch_shapes=[
+            pltpu.VMEM((2, 3, FULL, LANES), F32),
+            pltpu.VMEM((4, 2, 2, FULL, LANES), BF16),
+            pltpu.VMEM((4, 2, 4, 64, LANES), F32),
+            pltpu.VMEM((4, 2, 2, 4, 64, LANES), F32),
+        ]
+        + [pltpu.VMEM(t.shape, t.dtype) for t in tables]
+        + [
+            pltpu.VMEM(slc.shape, BF16),
+            pltpu.VMEM((2, 2, FULL, LANES), BF16),
             pltpu.VMEM((4, 4, 64, LANES), F32),
-            dma((2,)),
-            dma((2,)),
+            pltpu.SMEM(partner.shape, jnp.int32),
+            pltpu.SMEM(valid.shape, jnp.int32),
+            dma((8,)),
+            dma((4, 2)),
+            dma((4,)),
+            dma((4,)),
             dma((3, 2, 2)),
             dma((3, 2, 2)),
             dma((3, 2)),
             dma((3, 2)),
             dma((2, 2)),
             dma((2, 2)),
-            dma((2,)),
-            dma((2,)),
-        ],
+        ]
+        + work_shapes(),
         compiler_params=pltpu.CompilerParams(
-            collective_id=0, has_side_effects=True, vmem_limit_bytes=32 * 1024 * 1024
+            collective_id=0, has_side_effects=True, vmem_limit_bytes=60 * 1024 * 1024
         ),
-    )(slc)
+        name="interferograms",
+    )(partner, valid, slc, *tables)
 
 
 def untile(array):
@@ -525,8 +650,9 @@
 
 
 def shards(slc, partner, valid):
-    own, other = exchange(slc)
-    coherence, filtered = compute(partner, valid, own, other)
+    partner = partner.transpose(1, 2, 0)
+    valid = valid.transpose(1, 2, 0)
+    coherence, filtered = exchange(partner, valid, slc)
     return untile(coherence), untile(filtered)
 
 

time: 42.3 us -> 31.4 us (0.74)
  the two profiles are of different devices: /device:TPU:1 before, /device:TPU:24 now
where the time goes in v1:
time: 31.4 us; the launch traced here: 31.3 us
  Pallas kernels  26.9 us (86%)
  local copies, waits for them, and re-layouts  3.78 us (12%)
  between operations  0.65 us (2%)
    pallas_call x1, Pallas kernels, exchange(): pl.pallas_call(exchange_kernel, out_shape=(jax.ShapeDtypeStruct((4, 2, 4,...  26.9 us
    unnamed x4, local copies, waits for them, and re-layouts  3.78 us

profile of v1, /device:TPU:24, one launch (start us, length us, event | category | flops | bytes accessed | tf_op | source)
XLA Modules:
  0.0 31.3 jit_solution(16315221213083188881)
XLA Ops:
  0.6 26.9 %interferograms.1 = (f32[4,2,4,64,128]{4,3,2,1,0:T(8,128)}, f32[4,2,2,4,64,128]{5,4,3,2,1,0:T(8,128)}) custom-call(s32[1,2,4]{2,1,0:T(2,128)} %bitcast.15, s32[2,2,4]{2,1,0:T(2,128)} %bitcast.14, bf16[2,2,32,1024]{3,2,1,0:T(8,128)(2,1)} %slc_hbm.1, bf16[256,256]{1,0:T(8,128)(2,1)} %constant.10.clone.box_h, bf16[768,256]{1,0:T(8,128)(2,1)} %constant.11.clone.forward_h, ...), custom_call_target="tpu_custom_call" | custom-call | tf_op jit(solution)/shard_map/interferograms/pallas_call | solution.py:604
  27.5 0.0 copy-start
  27.6 2.5 %copy.12 = f32[4,2,32,1024]{3,2,1,0:T(8,128)} copy(f32[4,2,32,1024]{3,2,1,0:T(8,128)} %bitcast.13) | data formatting | bytes 2097152
  30.0 0.0 copy-done
  30.0 1.3 %copy.13 = f32[4,2,2,32,1024]{4,3,2,1,0:T(8,128)} copy(f32[4,2,2,32,1024]{4,3,2,1,0:T(8,128)S(1)} %bitcast.12) | data formatting | bytes 4194304
Async XLA Ops:
  27.5 2.5 %copy-start = (f32[4,2,2,4,64,128]{5,4,3,2,1,0:T(8,128)S(1)}, f32[4,2,2,4,64,128]{5,4,3,2,1,0:T(8,128)}, u32[]{:S(2)}) copy-start(f32[4,2,2,4,64,128]{5,4,3,2,1,0:T(8,128)} %get-tuple-element.5) | copy-start | bytes 6291460

commit v2 on v1

--- a/solution.py
+++ b/solution.py
@@ -25,6 +25,7 @@
 BODY = ROWS * SUBS
 FULL = EXT * SUBS
 TINY = 1.2e-38
+PAIRS = 8
 
 BOX_SCALE = 1.0 / 128.0
 BOX_RATIO = LOOK_A * LOOK_R / 128.0
@@ -148,18 +149,20 @@
     return jnp.dot(a, b, preferred_element_type=F32)
 
 
-def compute_pair(
-    first, start, end, own32, other, tables, put_coherence, put_filtered, box_in, ml, mid, spec_in, mags, mag_in
-):
-    box_t, forward_t, inverse_t, near_t, same_t = tables
+def row_masks(first, start, end):
+    masks = []
+    for r in range(EXT):
+        here = first + (r - HALO)
+        masks.append(jnp.where((here >= start) & (here < end), 1.0, 0.0).astype(F32))
+    return masks
+
+
+def multilook(first, start, end, own32, other, box_t, coherence, ml, box_in):
+    masks = row_masks(first, start, end)
     sub = lax.broadcasted_iota(jnp.int32, (SUBS, LANES), 0)
     lane = lax.broadcasted_iota(jnp.int32, (SUBS, LANES), 1)
     low_half = lane < LANES // 2
     inner = jnp.where(low_half, jnp.where(sub > 0, 1.0, 0.0), jnp.where(sub < SUBS - 1, 1.0, 0.0))
-    masks = []
-    for r in range(EXT):
-        here = first + (r - HALO)
-        masks.append(jnp.where((here >= start) & (here < end), 1.0, 0.0).astype(F32))
 
     kept = [[], [], [], []]
 
@@ -171,12 +174,12 @@
             r = 2 * q + half
             m = masks[r]
             one = pl.ds(r * SUBS, SUBS)
-            a_re = own32(0, one) * m
-            a_im = own32(1, one) * m
+            a_re = own32[0, one, :] * m
+            a_im = own32[1, one, :] * m
             c_re, c_im = row(c_re2, half), row(c_im2, half)
             kept[0].append(a_re * c_re + a_im * c_im)
             kept[1].append(a_im * c_re - a_re * c_im)
-            kept[2].append(own32(2, one) * m)
+            kept[2].append(own32[2, one, :] * m)
             kept[3].append((c_re * c_re + c_im * c_im) * m)
 
     add_products(0)
@@ -200,17 +203,21 @@
             r = g * 8 + n
             ml_f = []
             for f in range(4):
-                base = (f * 8 + n) * SUBS
-                own_part = y[base : base + SUBS, 0:LANES]
-                side = y[base : base + SUBS, LANES : 2 * LANES]
+                both = row(y, f * 8 + n)
+                side = both[:, LANES:]
                 side = jnp.where(low_half, pltpu.roll(side, 1, 0), pltpu.roll(side, SUBS - 1, 0))
-                ml_f.append(own_part + side * inner)
+                ml_f.append(both[:, 0:LANES] + side * inner)
             re, im, p1, p2 = ml_f
             ml[0, pl.ds(r * SUBS, SUBS), :] = re
             ml[1, pl.ds(r * SUBS, SUBS), :] = im
             size = root(re * re + im * im)
             down = lax.rsqrt(p1 * p2 + 1e-6 * BOX_RATIO * BOX_RATIO)
-            put_coherence(r, size * (down * masks[r + HALO]))
+            coherence[g, pl.ds(n, SUBS, stride=8), :] = size * (down * masks[r + HALO])
+
+
+def goldstein(first, start, end, tables, ml, filtered, mid, spec_in, mags, mag_in):
+    forward_t, inverse_t, near_t, same_t = tables
+    masks = row_masks(first, start, end)
 
     for b in range(8):
         x = [
@@ -298,47 +305,70 @@
         x = dft4(x, 1)
         for a in range(4):
             r = b + 8 * a
-            put_filtered(0, r, x[a][0] * masks[r + HALO])
-            put_filtered(1, r, x[a][1] * masks[r + HALO])
-
-
-def compute_round(rnd, first, partner, valid, own32, other, tables, coherence, filtered, scratch):
-    for i in range(2):
+            filtered[0, a, pl.ds(b, SUBS, stride=8), :] = x[a][0] * masks[r + HALO]
+            filtered[1, a, pl.ds(b, SUBS, stride=8), :] = x[a][1] * masks[r + HALO]
+
+
+def place_of(pair):
+    turn = lax.div(pair, 2)
+    return turn + lax.div(turn, 2) * (5 - 2 * turn), lax.rem(pair, 2)
+
+
+def compute_most(first, partner, valid, own32, other, tables, coherence, filtered, work, before, after):
+    box_in, ml, *rest = work
+    box_t, *filter_t = tables
+
+    def start(pair):
+        rnd, i = place_of(pair)
         which = partner[0, i, rnd]
 
-        def put_coherence(r, value, i=i):
-            coherence[i, r // 8, pl.ds(r % 8, SUBS, stride=8), :] = value
-
-        def put_filtered(c, r, value, i=i):
-            filtered[i, c, r // 8, pl.ds(r % 8, SUBS, stride=8), :] = value
-
-        compute_pair(
-            first,
-            valid[i, 0, rnd],
-            valid[i, 1, rnd],
-            lambda c, at, i=i: own32[i, c, at, :],
-            lambda c, at, which=which: jnp.where(which == 0, other[rnd, 0, c, at, :], other[rnd, 1, c, at, :]),
-            tables,
-            put_coherence,
-            put_filtered,
-            *[ref.at[i] for ref in scratch],
+        def image(c, at):
+            return jnp.where(which == 0, other[rnd, 0, c, at, :], other[rnd, 1, c, at, :])
+
+        multilook(
+            first, valid[i, 0, rnd], valid[i, 1, rnd], own32.at[i], image, box_t, coherence.at[rnd, i],
+            ml.at[lax.rem(pair, 3)], box_in,
         )
+
+    def finish(pair):
+        rnd, i = place_of(pair)
+        goldstein(
+            first, valid[i, 0, rnd], valid[i, 1, rnd], filter_t, ml.at[lax.rem(pair, 3)], filtered.at[rnd, i], *rest
+        )
+
+    def step(pair, carry):
+        before(pair)
+        finish(pair - 1)
+        start(pair)
+        after(pair - 1)
+        return carry
+
+    before(jnp.int32(0))
+    start(jnp.int32(0))
+    lax.fori_loop(1, PAIRS - 1, step, 0)
+    start(jnp.int32(PAIRS - 1))
 
 
 def work_shapes():
     return [
-        pltpu.VMEM((2, 2, 256, 2 * LANES), BF16),
-        pltpu.VMEM((2, 2, BODY, LANES), F32),
-        pltpu.VMEM((2, 2, BODY, LANES), F32),
-        pltpu.VMEM((2, BODY, 4 * LANES), BF16),
+        pltpu.VMEM((2, 256, 2 * LANES), BF16),
+        pltpu.VMEM((3, 2, BODY, LANES), F32),
+        *filter_shapes(),
+    ]
+
+
+def filter_shapes():
+    return [
         pltpu.VMEM((2, BODY, LANES), F32),
-        pltpu.VMEM((2, BODY, 2 * LANES), BF16),
+        pltpu.VMEM((BODY, 4 * LANES), BF16),
+        pltpu.VMEM((BODY, LANES), F32),
+        pltpu.VMEM((BODY, 2 * LANES), BF16),
     ]
 
 
 def exchange_kernel(
     partner_hbm, valid_hbm, slc_hbm, box_h, forward_h, inverse_h, near_h, same_h,
-    coherence_hbm, filtered_hbm,
+    coherence_hbm, filtered_hbm, ml_hbm,
     own32, other, coherence, filtered, box_t, forward_t, inverse_t, near_t, same_t,
     slc, own, lines, partner, valid, load_sem, out_sem,
     halo_send, halo_recv, main_send, main_recv, edge_send, edge_recv, fwd_send, fwd_recv, *work,
@@ -514,20 +544,16 @@
         for q in (0, EXT // 2 - 1):
             widen(i, q)
 
-    forwards = []
+    forwards = {}
     for i in range(2):
         for c in range(2):
-            mains[1, i, c].wait_recv()
-            forwards.append(
-                remote(
-                    other.at[1, i, c, body],
-                    other.at[2, i, c, body],
-                    fwd_send.at[i, c],
-                    fwd_recv.at[i, c],
-                    (onward, strip),
-                )
+            forwards[i, c] = remote(
+                other.at[1, i, c, body],
+                other.at[2, i, c, body],
+                fwd_send.at[i, c],
+                fwd_recv.at[i, c],
+                (onward, strip),
             )
-            forwards[-1].start()
     for i in range(2):
         for c in range(2):
             mains[0, i, c].wait_recv()
@@ -544,26 +570,31 @@
         copy.wait()
     tables = (box_t, forward_t, inverse_t, near_t, same_t)
 
-    def outputs(rnd):
+    def outputs(pair):
+        rnd, i = place_of(pair)
         return [
-            pltpu.make_async_copy(coherence.at[rnd], coherence_hbm.at[rnd], out_sem.at[rnd, 0]),
-            pltpu.make_async_copy(filtered.at[rnd], filtered_hbm.at[rnd], out_sem.at[rnd, 1]),
-        ]
-
-    def one_round(rnd, carry):
-        @pl.when(rnd == 1)
+            pltpu.make_async_copy(coherence.at[rnd, i], coherence_hbm.at[rnd, i], out_sem.at[0, pair]),
+            pltpu.make_async_copy(filtered.at[rnd, i], filtered_hbm.at[rnd, i], out_sem.at[1, pair]),
+        ]
+
+    def left_over(pair):
+        rnd, i = place_of(jnp.int32(pair))
+        return [
+            pltpu.make_async_copy(coherence.at[rnd, i], coherence_hbm.at[rnd, i], out_sem.at[0, pair]),
+            pltpu.make_async_copy(ml.at[pair % 3], ml_hbm.at[pair - PAIRS + 2], out_sem.at[1, pair]),
+        ]
+
+    def before(pair):
+        @pl.when(pair == 2)
         def _():
+            for i in range(2):
+                for c in range(2):
+                    mains[1, i, c].wait_recv()
+                    forwards[i, c].start()
             edges[1, 0].wait_recv()
             edges[1, 1].wait_recv()
 
-        @pl.when(rnd == 2)
-        def _():
-            for copy in forwards:
-                copy.wait_recv()
-            edges[2, 0].wait_recv()
-            edges[2, 1].wait_recv()
-
-        @pl.when(rnd == 3)
+        @pl.when(pair == 4)
         def _():
             for i in range(2):
                 for c in range(2):
@@ -571,14 +602,25 @@
             edges[3, 0].wait_recv()
             edges[3, 1].wait_recv()
 
-        compute_round(
-            rnd, strip * ROWS, partner, valid, own32, other, tables, coherence.at[rnd], filtered.at[rnd], work
-        )
-        for copy in outputs(rnd):
+        @pl.when(pair == 6)
+        def _():
+            for i in range(2):
+                for c in range(2):
+                    forwards[i, c].wait_recv()
+            edges[2, 0].wait_recv()
+            edges[2, 1].wait_recv()
+
+    def after(pair):
+        for copy in outputs(pair):
             copy.start()
-        return carry
-
-    lax.fori_loop(0, 4, one_round, 0)
+
+    ml = work[1]
+    compute_most(
+        strip * ROWS, partner, valid, own32, other, tables, coherence, filtered, work, before, after
+    )
+    for pair in (PAIRS - 2, PAIRS - 1):
+        for copy in left_over(pair):
+            copy.start()
 
     @pl.when(has_above)
     def _():
@@ -590,15 +632,17 @@
         for copy in down:
             copy.wait_send()
 
-    for copy in (*mains.values(), *edges.values(), *forwards):
+    for copy in (*mains.values(), *edges.values(), *forwards.values()):
         copy.wait_send()
-    for rnd in range(4):
-        for copy in outputs(rnd):
+    for pair in range(PAIRS - 2):
+        for copy in outputs(jnp.int32(pair)):
             copy.wait()
-
-
-def exchange(partner, valid, slc):
-    tables = [jnp.asarray(t) for t in make_tables()]
+    for pair in (PAIRS - 2, PAIRS - 1):
+        for copy in left_over(pair):
+            copy.wait()
+
+
+def exchange(partner, valid, slc, tables):
     hbm = pl.BlockSpec(memory_space=pltpu.HBM)
     dma = pltpu.SemaphoreType.DMA
     return pl.pallas_call(
@@ -606,9 +650,10 @@
         out_shape=(
             jax.ShapeDtypeStruct((4, 2, 4, 64, LANES), F32),
             jax.ShapeDtypeStruct((4, 2, 2, 4, 64, LANES), F32),
+            jax.ShapeDtypeStruct((2, 2, BODY, LANES), F32),
         ),
         in_specs=[hbm] * 8,
-        out_specs=(hbm, hbm),
+        out_specs=(hbm, hbm, hbm),
         scratch_shapes=[
             pltpu.VMEM((2, 3, FULL, LANES), F32),
             pltpu.VMEM((4, 2, 2, FULL, LANES), BF16),
@@ -623,7 +668,7 @@
             pltpu.SMEM(partner.shape, jnp.int32),
             pltpu.SMEM(valid.shape, jnp.int32),
             dma((8,)),
-            dma((4, 2)),
+            dma((2, PAIRS)),
             dma((4,)),
             dma((4,)),
             dma((3, 2, 2)),
@@ -641,6 +686,94 @@
     )(partner, valid, slc, *tables)
 
 
+def rest_kernel(
+    valid_hbm, done_coherence, done_filtered, ml_hbm, forward_h, inverse_h, near_h, same_h, coherence_hbm, filtered_hbm,
+    coherence, filtered, valid, ml, forward_t, inverse_t, near_t, same_t, load_sem, in_sem, out_sem, *work,
+):
+    first = lax.axis_index("strip") * ROWS
+    loads = []
+    for n, (src, dst) in enumerate(
+        [
+            (ml_hbm, ml),
+            (forward_h, forward_t),
+            (valid_hbm, valid),
+            (near_h, near_t),
+            (same_h, same_t),
+            (inverse_h, inverse_t),
+        ]
+    ):
+        loads.append(pltpu.make_async_copy(src, dst, load_sem.at[n]))
+        loads[-1].start()
+    ins, outs = [], []
+    for pair in range(PAIRS):
+        turn, i = pair // 2, pair % 2
+        rnd = (0, 1, 3, 2)[turn]
+        ins.append(pltpu.make_async_copy(done_coherence.at[rnd, i], coherence.at[rnd, i], in_sem.at[0, pair]))
+        outs.append(pltpu.make_async_copy(coherence.at[rnd, i], coherence_hbm.at[rnd, i], out_sem.at[0, pair]))
+        if pair < PAIRS - 2:
+            ins.append(pltpu.make_async_copy(done_filtered.at[rnd, i], filtered.at[rnd, i], in_sem.at[1, pair]))
+            outs.append(pltpu.make_async_copy(filtered.at[rnd, i], filtered_hbm.at[rnd, i], out_sem.at[1, pair]))
+    for copy in ins:
+        copy.start()
+    for copy in loads:
+        copy.wait()
+
+    def made(n):
+        rnd, i = place_of(n + PAIRS - 2)
+        return pltpu.make_async_copy(filtered.at[rnd, i], filtered_hbm.at[rnd, i], out_sem.at[1, n + PAIRS - 2])
+
+    def finish(n, carry):
+        @pl.when(n == 1)
+        def _():
+            for copy_in, copy_out in zip(ins, outs):
+                copy_in.wait()
+                copy_out.start()
+
+        rnd, i = place_of(n + PAIRS - 2)
+        goldstein(
+            first,
+            valid[i, 0, rnd],
+            valid[i, 1, rnd],
+            (forward_t, inverse_t, near_t, same_t),
+            ml.at[n],
+            filtered.at[rnd, i],
+            *work,
+        )
+        made(n).start()
+        return carry
+
+    lax.fori_loop(0, 2, finish, 0)
+    for copy in outs:
+        copy.wait()
+    for n in range(2):
+        made(jnp.int32(n)).wait()
+
+
+def rest(valid, coherence, filtered, ml, tables):
+    hbm = pl.BlockSpec(memory_space=pltpu.HBM)
+    dma = pltpu.SemaphoreType.DMA
+    return pl.pallas_call(
+        rest_kernel,
+        out_shape=(
+            jax.ShapeDtypeStruct(coherence.shape, F32),
+            jax.ShapeDtypeStruct(filtered.shape, F32),
+        ),
+        in_specs=[hbm] * 8,
+        out_specs=(hbm, hbm),
+        scratch_shapes=[
+            pltpu.VMEM(coherence.shape, F32),
+            pltpu.VMEM(filtered.shape, F32),
+            pltpu.SMEM(valid.shape, jnp.int32),
+            pltpu.VMEM(ml.shape, F32),
+        ]
+        + [pltpu.VMEM(t.shape, t.dtype) for t in tables]
+        + [dma((6,)), dma((2, PAIRS)), dma((2, PAIRS))]
+        + filter_shapes(),
+        compiler_params=pltpu.CompilerParams(vmem_limit_bytes=60 * 1024 * 1024),
+        name="rest",
+    )(valid, coherence, filtered, ml, *tables)
+
+
 def untile(array):
     lead = array.shape[:-3]
     array = array.reshape(lead + (4, 8, 8, LANES))
@@ -652,7 +785,9 @@
 def shards(slc, partner, valid):
     partner = partner.transpose(1, 2, 0)
     valid = valid.transpose(1, 2, 0)
-    coherence, filtered = exchange(partner, valid, slc)
+    tables = [jnp.asarray(t) for t in make_tables()]
+    coherence, filtered, ml = exchange(partner, valid, slc, tables)
+    coherence, filtered = rest(valid, coherence, filtered, ml, tables[1:])
     return untile(coherence), untile(filtered)
 
 

time: 31.4 us -> 31.2 us (level)
  local copies, waits for them, and re-layouts: 3.78 us -> 0 us
  Pallas kernels: 26.9 us -> 30.5 us
    pallas_call x0 -> x1, Pallas kernels: none -> 5.15 us  [rest(): pl.pallas_call(rest_kernel, out_shape=(jax.ShapeDtypeStruct(coherence.sha...]
    unnamed x4 -> x0, local copies, waits for them, and re-layouts: 3.78 us -> none
    pallas_call x1, Pallas kernels: 26.9 us -> 25.3 us  [exchange(): pl.pallas_call(exchange_kernel, out_shape=(jax.ShapeDtypeStruct((4, 2, 4,...]
where the time goes in v2:
time: 31.2 us; the launch traced here: 31.1 us
  Pallas kernels  30.5 us (98%)
  between operations  0.64 us (2%)
    pallas_call x1, Pallas kernels, exchange(): pl.pallas_call(exchange_kernel, out_shape=(jax.ShapeDtypeStruct((4, 2, 4,...  25.3 us
    pallas_call x1, Pallas kernels, rest(): pl.pallas_call(rest_kernel, out_shape=(jax.ShapeDtypeStruct(coherence.sha...  5.15 us

profile of v2, /device:TPU:24, one launch (start us, length us, event | category | flops | bytes accessed | tf_op | source)
XLA Modules:
  0.0 31.1 jit_solution(14470333098641905335)
XLA Ops:
  0.6 25.3 %interferograms.1 = (f32[4,2,4,64,128]{4,3,2,1,0:T(8,128)}, f32[4,2,2,4,64,128]{5,4,3,2,1,0:T(8,128)}, f32[2,2,256,128]{3,2,1,0:T(8,128)}) custom-call(s32[1,2,4]{2,1,0:T(2,128)} %bitcast.14, s32[2,2,4]{2,1,0:T(2,128)} %bitcast.12, bf16[2,2,32,1024]{3,2,1,0:T(8,128)(2,1)} %slc_hbm.1, bf16[256,256]{1,0:T(8,128)(2,1)} %constant.10.clone.box_h, ...), custom_call_target="tpu_custom_call" | custom-call | tf_op jit(solution)/shard_map/interferograms/pallas_call | solution.py:648
  25.9 5.1 %rest.1 = (f32[4,2,4,64,128]{4,3,2,1,0:T(8,128)}, f32[4,2,2,4,64,128]{5,4,3,2,1,0:T(8,128)}) custom-call(s32[2,2,4]{2,1,0:T(2,128)} %bitcast.13, f32[4,2,4,64,128]{4,3,2,1,0:T(8,128)} %get-tuple-element.7.done_coherence, f32[4,2,2,4,64,128]{5,4,3,2,1,0:T(8,128)} %get-tuple-element.8.done_filtered, f32[2,2,256,128]{3,2,1,0:T(8,128)} %get-tuple-element.9.ml_hbm, ...), custom_call_target="tpu_custom_call" | custom-call | tf_op jit(solution)/shard_map/rest/pallas_call | solution.py:755

commit v3 on v1

--- a/solution.py
+++ b/solution.py
@@ -148,69 +148,135 @@
     return jnp.dot(a, b, preferred_element_type=F32)
 
 
-def compute_pair(
-    first, start, end, own32, other, tables, put_coherence, put_filtered, box_in, ml, mid, spec_in, mags, mag_in
-):
-    box_t, forward_t, inverse_t, near_t, same_t = tables
-    sub = lax.broadcasted_iota(jnp.int32, (SUBS, LANES), 0)
-    lane = lax.broadcasted_iota(jnp.int32, (SUBS, LANES), 1)
-    low_half = lane < LANES // 2
-    inner = jnp.where(low_half, jnp.where(sub > 0, 1.0, 0.0), jnp.where(sub < SUBS - 1, 1.0, 0.0))
+def row_masks(first, start, end):
     masks = []
     for r in range(EXT):
         here = first + (r - HALO)
         masks.append(jnp.where((here >= start) & (here < end), 1.0, 0.0).astype(F32))
-
-    kept = [[], [], [], []]
+    return masks
+
+
+def added(*terms):
+    total = None
+    for term in terms:
+        if term is not None:
+            total = term if total is None else total + term
+    return total
+
+
+class Look:
+    def __init__(self, first, start, end, own32, other, box_t, coherence, ml, part):
+        self.masks = row_masks(first, start, end)
+        self.own32, self.other, self.box_t = own32, other, box_t
+        self.coherence, self.ml, self.part = coherence, ml, part
+        sub = lax.broadcasted_iota(jnp.int32, (SUBS, LANES), 0)
+        lane = lax.broadcasted_iota(jnp.int32, (SUBS, LANES), 1)
+        self.low_half = lane < LANES // 2
+        self.inner = jnp.where(
+            self.low_half, jnp.where(sub > 0, 1.0, 0.0), jnp.where(sub < SUBS - 1, 1.0, 0.0)
+        )
+
+    def products(self, q):
+        at = pl.ds(q * 16, 16)
+        c_re2 = self.other(0, at).astype(F32)
+        c_im2 = self.other(1, at).astype(F32)
+        rows = []
+        for half in range(2):
+            m = self.masks[2 * q + half]
+            one = pl.ds((2 * q + half) * SUBS, SUBS)
+            a_re = self.own32[0, one, :] * m
+            a_im = self.own32[1, one, :] * m
+            c_re, c_im = row(c_re2, half), row(c_im2, half)
+            rows.append(
+                (
+                    a_re * c_re + a_im * c_im,
+                    a_im * c_re - a_re * c_im,
+                    self.own32[2, one, :] * m,
+                    (c_re * c_re + c_im * c_im) * m,
+                )
+            )
+        return rows
+
+    def boxed(self, y, place):
+        both = row(y, place)
+        side = both[:, LANES:]
+        side = jnp.where(self.low_half, pltpu.roll(side, 1, 0), pltpu.roll(side, SUBS - 1, 0))
+        return both[:, 0:LANES] + side * self.inner
+
+    def put(self, r, re, im, p1, p2):
+        self.ml[0, pl.ds(r * SUBS, SUBS), :] = re
+        self.ml[1, pl.ds(r * SUBS, SUBS), :] = im
+        size = root(re * re + im * im)
+        down = lax.rsqrt(p1 * p2 + 1e-6 * BOX_RATIO * BOX_RATIO)
+        self.coherence[r // 8, pl.ds(r % 8, SUBS, stride=8), :] = size * (down * self.masks[r + HALO])
+
+
+EDGE_ROWS = (0, 1, ROWS - 2, ROWS - 1)
+
+
+def multilook(look, box_in):
+    kept = [[None, None] for _ in range(4)]
 
     def add_products(q):
-        at = pl.ds(q * 16, 16)
-        c_re2 = other(0, at).astype(F32)
-        c_im2 = other(1, at).astype(F32)
-        for half in range(2):
-            r = 2 * q + half
-            m = masks[r]
-            one = pl.ds(r * SUBS, SUBS)
-            a_re = own32(0, one) * m
-            a_im = own32(1, one) * m
-            c_re, c_im = row(c_re2, half), row(c_im2, half)
-            kept[0].append(a_re * c_re + a_im * c_im)
-            kept[1].append(a_im * c_re - a_re * c_im)
-            kept[2].append(own32(2, one) * m)
-            kept[3].append((c_re * c_re + c_im * c_im) * m)
-
-    add_products(0)
+        for fields in look.products(q):
+            for f in range(4):
+                kept[f].append(fields[f])
+
     add_products(1)
-    two = [[kept[f][n] + kept[f][n + 1] for n in range(3)] for f in range(4)]
+    two = [[None, kept[f][2], kept[f][2] + kept[f][3]] for f in range(4)]
     for g in range(ROWS // SUBS):
         for q in range(4):
-            add_products(2 + g * 4 + q)
+            tile = 2 + g * 4 + q
+            if tile < EXT // 2 - 1:
+                add_products(tile)
+            else:
+                for f in range(4):
+                    kept[f] += [None, None]
             for f in range(4):
                 sums = []
                 for half in range(2):
                     r = g * 8 + q * 2 + half
-                    two[f].append(kept[f][r + 3] + kept[f][r + 4])
-                    sums.append(kept[f][r] + (two[f][r + 1] + two[f][r + 3]))
+                    two[f].append(added(kept[f][r + 3], kept[f][r + 4]))
+                    sums.append(added(kept[f][r], added(two[f][r + 1], two[f][r + 3])))
                 high, low = split(pair_up(*sums))
                 at = pl.ds(f * 64 + q * 16, 16)
                 box_in[g % 2, at, 0:LANES] = high
                 box_in[g % 2, at, LANES : 2 * LANES] = low
-        y = dot(box_in[g % 2], box_t[...])
+        y = dot(box_in[g % 2], look.box_t[...])
         for n in range(8):
             r = g * 8 + n
-            ml_f = []
-            for f in range(4):
-                base = (f * 8 + n) * SUBS
-                own_part = y[base : base + SUBS, 0:LANES]
-                side = y[base : base + SUBS, LANES : 2 * LANES]
-                side = jnp.where(low_half, pltpu.roll(side, 1, 0), pltpu.roll(side, SUBS - 1, 0))
-                ml_f.append(own_part + side * inner)
-            re, im, p1, p2 = ml_f
-            ml[0, pl.ds(r * SUBS, SUBS), :] = re
-            ml[1, pl.ds(r * SUBS, SUBS), :] = im
-            size = root(re * re + im * im)
-            down = lax.rsqrt(p1 * p2 + 1e-6 * BOX_RATIO * BOX_RATIO)
-            put_coherence(r, size * (down * masks[r + HALO]))
+            fields = [look.boxed(y, f * 8 + n) for f in range(4)]
+            if r in EDGE_ROWS:
+                at = pl.ds(EDGE_ROWS.index(r) * SUBS, SUBS)
+                look.ml[0, pl.ds(r * SUBS, SUBS), :] = fields[0]
+                look.ml[1, pl.ds(r * SUBS, SUBS), :] = fields[1]
+                look.part[0, at, :] = fields[2]
+                look.part[1, at, :] = fields[3]
+            else:
+                look.put(r, *fields)
+
+
+def add_halo(look, halo_in):
+    before = look.products(0)
+    after = look.products(EXT // 2 - 1)
+    for f in range(4):
+        for n, rows in enumerate(
+            [(before[0][f] + before[1][f], before[1][f]), (after[0][f], after[0][f] + after[1][f])]
+        ):
+            high, low = split(pair_up(*rows))
+            at = pl.ds(f * 32 + n * 16, 16)
+            halo_in[at, 0:LANES] = high
+            halo_in[at, LANES : 2 * LANES] = low
+    y = dot(halo_in[...], look.box_t[...])
+    for n, r in enumerate(EDGE_ROWS):
+        at, here = pl.ds(n * SUBS, SUBS), pl.ds(r * SUBS, SUBS)
+        held = [look.ml[0, here, :], look.ml[1, here, :], look.part[0, at, :], look.part[1, at, :]]
+        look.put(r, *[held[f] + look.boxed(y, f * 4 + n) for f in range(4)])
+
+
+def goldstein(first, start, end, tables, ml, filtered, mid, spec_in, mags, mag_in):
+    forward_t, inverse_t, near_t, same_t = tables
+    masks = row_masks(first, start, end)
 
     for b in range(8):
         x = [
@@ -298,37 +364,76 @@
         x = dft4(x, 1)
         for a in range(4):
             r = b + 8 * a
-            put_filtered(0, r, x[a][0] * masks[r + HALO])
-            put_filtered(1, r, x[a][1] * masks[r + HALO])
-
-
-def compute_round(rnd, first, partner, valid, own32, other, tables, coherence, filtered, scratch):
-    for i in range(2):
+            filtered[0, a, pl.ds(b, SUBS, stride=8), :] = x[a][0] * masks[r + HALO]
+            filtered[1, a, pl.ds(b, SUBS, stride=8), :] = x[a][1] * masks[r + HALO]
+
+
+def place_of(turn):
+    return turn + lax.div(turn, 2) * (5 - 2 * turn)
+
+
+def compute_all(
+    first, partner, valid, own32, other, tables, coherence, filtered, work, before_look, before_halo, after
+):
+    box_in, halo_in, ml, part, *rest = work
+    box_t, *filter_t = tables
+    turns = 4
+
+    def look_of(rnd, i):
         which = partner[0, i, rnd]
 
-        def put_coherence(r, value, i=i):
-            coherence[i, r // 8, pl.ds(r % 8, SUBS, stride=8), :] = value
-
-        def put_filtered(c, r, value, i=i):
-            filtered[i, c, r // 8, pl.ds(r % 8, SUBS, stride=8), :] = value
-
-        compute_pair(
-            first,
-            valid[i, 0, rnd],
-            valid[i, 1, rnd],
-            lambda c, at, i=i: own32[i, c, at, :],
-            lambda c, at, which=which: jnp.where(which == 0, other[rnd, 0, c, at, :], other[rnd, 1, c, at, :]),
-            tables,
-            put_coherence,
-            put_filtered,
-            *[ref.at[i] for ref in scratch],
+        def image(c, at):
+            return jnp.where(which == 0, other[rnd, 0, c, at, :], other[rnd, 1, c, at, :])
+
+        return Look(
+            first, valid[i, 0, rnd], valid[i, 1, rnd], own32.at[i], image, box_t, coherence.at[rnd, i],
+            ml.at[rnd, i], part.at[rnd, i],
         )
+
+    def look_turn(turn):
+        before_look(turn)
+        rnd = place_of(turn)
+        for i in range(2):
+            multilook(look_of(rnd, i), box_in.at[i])
+
+    def halo_turn(turn):
+        before_halo(turn)
+        rnd = place_of(turn)
+        for i in range(2):
+            add_halo(look_of(rnd, i), halo_in.at[i])
+
+    def filter_turn(turn):
+        halo_turn(turn)
+        rnd = place_of(turn)
+        for i in range(2):
+            goldstein(
+                first, valid[i, 0, rnd], valid[i, 1, rnd], filter_t, ml.at[rnd, i], filtered.at[rnd, i],
+                *[ref.at[i] for ref in rest],
+            )
+        after(turn)
+
+    def step(n, carry):
+        looks = (n < turns - 1) | (n == turns + 1)
+
+        @pl.when(looks)
+        def _():
+            look_turn(jnp.minimum(n, turns - 1))
+
+        @pl.when(jnp.logical_not(looks))
+        def _():
+            filter_turn(n - (turns - 1) - lax.div(n, turns + 1))
+
+        return carry
+
+    lax.fori_loop(0, 2 * turns, step, 0)
 
 
 def work_shapes():
     return [
         pltpu.VMEM((2, 2, 256, 2 * LANES), BF16),
-        pltpu.VMEM((2, 2, BODY, LANES), F32),
+        pltpu.VMEM((2, 128, 2 * LANES), BF16),
+        pltpu.VMEM((4, 2, 2, BODY, LANES), F32),
+        pltpu.VMEM((4, 2, 2, 4 * SUBS, LANES), F32),
         pltpu.VMEM((2, 2, BODY, LANES), F32),
         pltpu.VMEM((2, BODY, 4 * LANES), BF16),
         pltpu.VMEM((2, BODY, LANES), F32),
@@ -341,7 +446,7 @@
     coherence_hbm, filtered_hbm,
     own32, other, coherence, filtered, box_t, forward_t, inverse_t, near_t, same_t,
     slc, own, lines, partner, valid, load_sem, out_sem,
-    halo_send, halo_recv, main_send, main_recv, edge_send, edge_recv, fwd_send, fwd_recv, *work,
+    far_sem, halo_send, halo_recv, main_send, main_recv, edge_send, edge_recv, fwd_send, fwd_recv, *work,
 ):
     date = lax.axis_index("date")
     strip = lax.axis_index("strip")
@@ -358,6 +463,10 @@
     mate, onward = xor(1), xor(6)
     partners = {0: mate, 1: xor(2), 2: xor(4), 3: xor(8)}
     has_above, has_below = strip > 0, strip < n_strip - 1
+    far_upper, far_lower = strip == n_strip // 2 - 1, strip == n_strip // 2
+    upper_asks = date < lax.axis_size("date") * 3 // 4
+    upper_answers = jnp.logical_not(upper_asks)
+    asks = (far_upper & upper_asks) | (far_lower & upper_answers)
 
     loads = []
     for n, (src, dst) in enumerate(
@@ -380,12 +489,12 @@
     def greet(device):
         pl.semaphore_signal(barrier, inc=1, device_id=device, device_id_type=MESH)
 
-    @pl.when(has_above)
+    @pl.when(has_above & jnp.logical_not(far_lower & upper_asks))
     def _():
         greet((date, strip - 1))
         greet((mate, strip - 1))
 
-    @pl.when(has_below)
+    @pl.when(has_below & jnp.logical_not(far_upper & upper_answers))
     def _():
         greet((date, strip + 1))
         greet((mate, strip + 1))
@@ -446,7 +555,7 @@
         remote(own.at[:, :, last_rows], own.at[:, :, top], halo_send.at[1], halo_recv.at[1], (date, strip + 1)),
         remote(own.at[:, :, last_rows], other.at[0, :, :, top], halo_send.at[3], halo_recv.at[3], (mate, strip + 1)),
     ]
-    inside = has_above & has_below
+    inside = has_above & has_below & jnp.logical_not(asks)
 
     @pl.when(inside)
     def _():
@@ -456,15 +565,25 @@
     def _():
         pl.semaphore_wait(barrier, 7)
 
-    @pl.when(has_above)
+    @pl.when(has_above & jnp.logical_not(far_lower & asks))
     def _():
         for copy in up:
             copy.start()
 
-    @pl.when(has_below)
+    @pl.when(has_below & jnp.logical_not(far_upper & asks))
     def _():
         for copy in down:
             copy.start()
+
+    @pl.when(far_lower & upper_asks)
+    def _():
+        for device in (date, mate):
+            pl.semaphore_signal(far_sem, inc=1, device_id=(device, strip - 1), device_id_type=MESH)
+
+    @pl.when(far_upper & upper_answers)
+    def _():
+        for device in (date, mate):
+            pl.semaphore_signal(far_sem, inc=1, device_id=(device, strip + 1), device_id_type=MESH)
 
     mains = {}
     for i in range(2):
@@ -491,15 +610,16 @@
         for q in range(1, EXT // 2 - 1):
             widen(i, q)
 
-    @pl.when(has_below)
-    def _():
-        up[0].wait_recv()
-
-    @pl.when(has_above)
-    def _():
-        down[0].wait_recv()
-
-    edges = {}
+    forwards, edges = {}, {}
+    for i in range(2):
+        for c in range(2):
+            forwards[i, c] = remote(
+                other.at[1, i, c, body],
+                other.at[2, i, c, body],
+                fwd_send.at[i, c],
+                fwd_recv.at[i, c],
+                (onward, strip),
+            )
     for n, r in enumerate((1, 2, 3)):
         for side, at in enumerate((top, bottom)):
             edges[r, side] = remote(
@@ -509,76 +629,109 @@
                 edge_recv.at[n, side],
                 (partners[r], strip),
             )
-            edges[r, side].start()
-    for i in range(2):
-        for q in (0, EXT // 2 - 1):
-            widen(i, q)
-
-    forwards = []
-    for i in range(2):
-        for c in range(2):
-            mains[1, i, c].wait_recv()
-            forwards.append(
-                remote(
-                    other.at[1, i, c, body],
-                    other.at[2, i, c, body],
-                    fwd_send.at[i, c],
-                    fwd_recv.at[i, c],
-                    (onward, strip),
-                )
-            )
-            forwards[-1].start()
-    for i in range(2):
-        for c in range(2):
-            mains[0, i, c].wait_recv()
-
-    @pl.when(has_below)
-    def _():
-        up[1].wait_recv()
-
-    @pl.when(has_above)
-    def _():
-        down[1].wait_recv()
-
-    for copy in loads[1:]:
-        copy.wait()
-    tables = (box_t, forward_t, inverse_t, near_t, same_t)
-
-    def outputs(rnd):
-        return [
-            pltpu.make_async_copy(coherence.at[rnd], coherence_hbm.at[rnd], out_sem.at[rnd, 0]),
-            pltpu.make_async_copy(filtered.at[rnd], filtered_hbm.at[rnd], out_sem.at[rnd, 1]),
-        ]
-
-    def one_round(rnd, carry):
-        @pl.when(rnd == 1)
-        def _():
-            edges[1, 0].wait_recv()
-            edges[1, 1].wait_recv()
-
-        @pl.when(rnd == 2)
-        def _():
-            for copy in forwards:
-                copy.wait_recv()
-            edges[2, 0].wait_recv()
-            edges[2, 1].wait_recv()
-
-        @pl.when(rnd == 3)
+
+    far = far_upper | far_lower
+
+    def take_halo():
+        @pl.when(has_below)
+        def _():
+            up[0].wait_recv()
+
+        @pl.when(has_above)
+        def _():
+            down[0].wait_recv()
+
+        for copy in edges.values():
+            copy.start()
+        for i in range(2):
+            for q in (0, EXT // 2 - 1):
+                widen(i, q)
+
+    def send_far():
+        @pl.when(asks)
+        def _():
+            pl.semaphore_wait(far_sem, 2)
+
+        @pl.when(far_upper & asks)
+        def _():
+            for copy in down:
+                copy.start()
+
+        @pl.when(far_lower & asks)
+        def _():
+            for copy in up:
+                copy.start()
+
+    def before_look(turn):
+        @pl.when(turn == 0)
+        def _():
+            for i in range(2):
+                for c in range(2):
+                    mains[0, i, c].wait_recv()
+            for copy in loads[1:]:
+                copy.wait()
+
+        @pl.when(turn == 1)
+        def _():
+            @pl.when(jnp.logical_not(far))
+            def _():
+                take_halo()
+
+            for i in range(2):
+                for c in range(2):
+                    mains[1, i, c].wait_recv()
+                    forwards[i, c].start()
+                if i == 0:
+                    send_far()
+
+        @pl.when(turn == 2)
         def _():
             for i in range(2):
                 for c in range(2):
                     mains[3, i, c].wait_recv()
-            edges[3, 0].wait_recv()
-            edges[3, 1].wait_recv()
-
-        compute_round(
-            rnd, strip * ROWS, partner, valid, own32, other, tables, coherence.at[rnd], filtered.at[rnd], work
-        )
-        for copy in outputs(rnd):
+
+        @pl.when(turn == 3)
+        def _():
+            for copy in forwards.values():
+                copy.wait_recv()
+
+    def before_halo(turn):
+        @pl.when(turn == 0)
+        def _():
+            @pl.when(far)
+            def _():
+                take_halo()
+
+            @pl.when(has_below)
+            def _():
+                up[1].wait_recv()
+
+            @pl.when(has_above)
+            def _():
+                down[1].wait_recv()
+
+        for n, r in ((1, 1), (2, 3), (3, 2)):
+
+            @pl.when(turn == n)
+            def _(r=r):
+                edges[r, 0].wait_recv()
+                edges[r, 1].wait_recv()
+
+    def outputs(turn):
+        rnd = place_of(turn)
+        return [
+            pltpu.make_async_copy(coherence.at[rnd], coherence_hbm.at[rnd], out_sem.at[0, turn]),
+            pltpu.make_async_copy(filtered.at[rnd], filtered_hbm.at[rnd], out_sem.at[1, turn]),
+        ]
+
+    def after(turn):
+        for copy in outputs(turn):
             copy.start()
-        return carry
-
-    lax.fori_loop(0, 4, one_round, 0)
+
+    tables = (box_t, forward_t, inverse_t, near_t, same_t)
+    compute_all(
+        strip * ROWS, partner, valid, own32, other, tables, coherence, filtered, work, before_look, before_halo, after
+    )
 
     @pl.when(has_above)
     def _():
@@ -590,15 +743,14 @@
         for copy in down:
             copy.wait_send()
 
-    for copy in (*mains.values(), *edges.values(), *forwards):
+    for copy in (*mains.values(), *edges.values(), *forwards.values()):
         copy.wait_send()
-    for rnd in range(4):
-        for copy in outputs(rnd):
+    for turn in range(4):
+        for copy in outputs(jnp.int32(turn)):
             copy.wait()
 
 
-def exchange(partner, valid, slc):
-    tables = [jnp.asarray(t) for t in make_tables()]
+def exchange(partner, valid, slc, tables):
     hbm = pl.BlockSpec(memory_space=pltpu.HBM)
     dma = pltpu.SemaphoreType.DMA
     return pl.pallas_call(
@@ -623,7 +775,8 @@
             pltpu.SMEM(partner.shape, jnp.int32),
             pltpu.SMEM(valid.shape, jnp.int32),
             dma((8,)),
-            dma((4, 2)),
+            dma((2, 4)),
+            pltpu.SemaphoreType.REGULAR,
             dma((4,)),
             dma((4,)),
             dma((3, 2, 2)),
@@ -641,6 +794,46 @@
     )(partner, valid, slc, *tables)
 
 
+def hand_on_kernel(done_coherence, done_filtered, coherence_hbm, filtered_hbm, coherence, filtered, in_sem, out_sem):
+    ins, outs = [], []
+    for rnd in range(4):
+        for i in range(2):
+            for n, (src, by, dst) in enumerate(
+                [(done_filtered, filtered, filtered_hbm), (done_coherence, coherence, coherence_hbm)]
+            ):
+                ins.append(pltpu.make_async_copy(src.at[rnd, i], by.at[rnd, i], in_sem.at[n, rnd, i]))
+                outs.append(pltpu.make_async_copy(by.at[rnd, i], dst.at[rnd, i], out_sem.at[n, rnd, i]))
+    for copy in ins:
+        copy.start()
+    for copy_in, copy_out in zip(ins, outs):
+        copy_in.wait()
+        copy_out.start()
+    for copy in outs:
+        copy.wait()
+
+
+def hand_on(coherence, filtered):
+    hbm = pl.BlockSpec(memory_space=pltpu.HBM)
+    dma = pltpu.SemaphoreType.DMA
+    return pl.pallas_call(
+        hand_on_kernel,
+        out_shape=(
+            jax.ShapeDtypeStruct(coherence.shape, F32),
+            jax.ShapeDtypeStruct(filtered.shape, F32),
+        ),
+        in_specs=[hbm, hbm],
+        out_specs=(hbm, hbm),
+        scratch_shapes=[
+            pltpu.VMEM(coherence.shape, F32),
+            pltpu.VMEM(filtered.shape, F32),
+            dma((2, 4, 2)),
+            dma((2, 4, 2)),
+        ],
+        compiler_params=pltpu.CompilerParams(vmem_limit_bytes=60 * 1024 * 1024),
+        name="hand_on",
+    )(coherence, filtered)
+
+
 def untile(array):
     lead = array.shape[:-3]
     array = array.reshape(lead + (4, 8, 8, LANES))
@@ -652,7 +845,8 @@
 def shards(slc, partner, valid):
     partner = partner.transpose(1, 2, 0)
     valid = valid.transpose(1, 2, 0)
-    coherence, filtered = exchange(partner, valid, slc)
+    tables = [jnp.asarray(t) for t in make_tables()]
+    coherence, filtered = hand_on(*exchange(partner, valid, slc, tables))
     return untile(coherence), untile(filtered)
 
 

time: 31.4 us -> 28.9 us (0.920)
  the two profiles are of different devices: /device:TPU:24 before, /device:TPU:88 now
where the time goes in v3:
time: 28.9 us; the launch traced here: 28.8 us
  Pallas kernels  28.1 us (97%)
  between operations  0.64 us (2%)
    pallas_call x1, Pallas kernels, exchange(): pl.pallas_call(exchange_kernel, out_shape=(jax.ShapeDtypeStruct((4, 2, 4,...  25.2 us
    pallas_call x1, Pallas kernels, hand_on(): pl.pallas_call(hand_on_kernel, out_shape=(jax.ShapeDtypeStruct(coherence....  2.89 us

profile of v3, /device:TPU:88, one launch (start us, length us, event | category | flops | bytes accessed | tf_op | source)
XLA Modules:
  0.0 28.8 jit_solution(17720064583255755165)
XLA Ops:
  0.6 25.2 %interferograms.1 = (f32[4,2,4,64,128]{4,3,2,1,0:T(8,128)}, f32[4,2,2,4,64,128]{5,4,3,2,1,0:T(8,128)}) custom-call(s32[1,2,4]{2,1,0:T(2,128)} %bitcast.13, s32[2,2,4]{2,1,0:T(2,128)} %bitcast.12, bf16[2,2,32,1024]{3,2,1,0:T(8,128)(2,1)} %slc_hbm.1, bf16[256,256]{1,0:T(8,128)(2,1)} %constant.10.clone.box_h, bf16[768,256]{1,0:T(8,128)(2,1)} %constant.11.clone.forward_h, ...), custom_call_target="tpu_custom_call" | custom-call | tf_op jit(solution)/shard_map/interferograms/pallas_call | solution.py:756
  25.9 2.9 %hand_on.1 = (f32[4,2,4,64,128]{4,3,2,1,0:T(8,128)}, f32[4,2,2,4,64,128]{5,4,3,2,1,0:T(8,128)}) custom-call(f32[4,2,4,64,128]{4,3,2,1,0:T(8,128)} %get-tuple-element.6.done_coherence, f32[4,2,2,4,64,128]{5,4,3,2,1,0:T(8,128)} %get-tuple-element.7.done_filtered), custom_call_target="tpu_custom_call" | custom-call | tf_op jit(solution)/shard_map/hand_on/pallas_call | solution.py:818

commit v4 on v3

--- a/solution.py
+++ b/solution.py
@@ -242,7 +242,7 @@
                 at = pl.ds(f * 64 + q * 16, 16)
                 box_in[g % 2, at, 0:LANES] = high
                 box_in[g % 2, at, LANES : 2 * LANES] = low
-        y = dot(box_in[g % 2], look.box_t[...])
+        y = yield box_in[g % 2], look.box_t
         for n in range(8):
             r = g * 8 + n
             fields = [look.boxed(y, f * 8 + n) for f in range(4)]
@@ -267,7 +267,7 @@
             at = pl.ds(f * 32 + n * 16, 16)
             halo_in[at, 0:LANES] = high
             halo_in[at, LANES : 2 * LANES] = low
-    y = dot(halo_in[...], look.box_t[...])
+    y = yield halo_in[...], look.box_t
     for n, r in enumerate(EDGE_ROWS):
         at, here = pl.ds(n * SUBS, SUBS), pl.ds(r * SUBS, SUBS)
         held = [look.ml[0, here, :], look.ml[1, here, :], look.part[0, at, :], look.part[1, at, :]]
@@ -306,7 +306,7 @@
             put_split(k1 * 8 + k2, x[k2 : k2 + 2])
 
     both = spec_in[...]
-    s = dot(jnp.concatenate([both, both[:, 0 : 2 * LANES]], 1), forward_t[...])
+    s = yield jnp.concatenate([both, both[:, 0 : 2 * LANES]], 1), forward_t
     for p in range(ROWS):
         at = pl.ds(p * SUBS, SUBS)
         re, im = row(s, p)[:, 0:LANES], row(s, p)[:, LANES:]
@@ -332,9 +332,10 @@
         mag_in[pl.ds(p * SUBS, 16), 0:LANES] = high
         mag_in[pl.ds(p * SUBS, 16), LANES:] = low
     high, low = split(pair_up(total, total))
-    tile_sum = dot(jnp.concatenate([high, low], 1), same_t[...])[0:SUBS]
+    tile_sum = yield jnp.concatenate([high, low], 1), same_t
+    tile_sum = tile_sum[0:SUBS]
     inv = (1.0 / 9.0) / (tile_sum * (1.0 / (3 * PATCH * PATCH)) + 1e-6 / (PATCH * PATCH))
-    smooth = dot(mag_in[...], near_t[...])
+    smooth = yield mag_in[...], near_t
     for p in range(0, ROWS, 2):
         parts = []
         for n in (p, p + 1):
@@ -344,7 +345,7 @@
         put_split(p, parts)
 
     both = spec_in[...]
-    s = dot(jnp.concatenate([both, both[:, 0 : 2 * LANES]], 1), inverse_t[...])
+    s = yield jnp.concatenate([both, both[:, 0 : 2 * LANES]], 1), inverse_t
     for k1 in range(4):
         x = [
             (row(s, k1 * 8 + k2)[:, 0:LANES], row(s, k1 * 8 + k2)[:, LANES:])
@@ -372,6 +373,20 @@
     return turn + lax.div(turn, 2) * (5 - 2 * turn)
 
 
+def together(parts):
+    asked = [next(part) for part in parts]
+    while asked:
+        made = dot(jnp.concatenate([left for left, _ in asked], 0), asked[0][1][...])
+        rows = made.shape[0] // len(parts)
+        following = []
+        for n, part in enumerate(parts):
+            try:
+                following.append(part.send(made[n * rows : (n + 1) * rows]))
+            except StopIteration:
+                pass
+        asked = following
+
+
 def compute_all(
     first, partner, valid, own32, other, tables, coherence, filtered, work, before_look, before_halo, after
 ):
@@ -393,23 +408,25 @@
     def look_turn(turn):
         before_look(turn)
         rnd = place_of(turn)
-        for i in range(2):
-            multilook(look_of(rnd, i), box_in.at[i])
+        together([multilook(look_of(rnd, i), box_in.at[i]) for i in range(2)])
 
     def halo_turn(turn):
         before_halo(turn)
         rnd = place_of(turn)
-        for i in range(2):
-            add_halo(look_of(rnd, i), halo_in.at[i])
+        together([add_halo(look_of(rnd, i), halo_in.at[i]) for i in range(2)])
 
     def filter_turn(turn):
         halo_turn(turn)
         rnd = place_of(turn)
-        for i in range(2):
-            goldstein(
-                first, valid[i, 0, rnd], valid[i, 1, rnd], filter_t, ml.at[rnd, i], filtered.at[rnd, i],
-                *[ref.at[i] for ref in rest],
-            )
+        together(
+            [
+                goldstein(
+                    first, valid[i, 0, rnd], valid[i, 1, rnd], filter_t, ml.at[rnd, i], filtered.at[rnd, i],
+                    *[ref.at[i] for ref in rest],
+                )
+                for i in range(2)
+            ]
+        )
         after(turn)
 
     def step(n, carry):
@@ -464,9 +481,24 @@
     partners = {0: mate, 1: xor(2), 2: xor(4), 3: xor(8)}
     has_above, has_below = strip > 0, strip < n_strip - 1
     far_upper, far_lower = strip == n_strip // 2 - 1, strip == n_strip // 2
-    upper_asks = date < lax.axis_size("date") * 3 // 4
-    upper_answers = jnp.logical_not(upper_asks)
-    asks = (far_upper & upper_asks) | (far_lower & upper_answers)
+
+    barrier = pltpu.get_barrier_semaphore()
+
+    def greet(device):
+        pl.semaphore_signal(barrier, inc=1, device_id=device, device_id_type=MESH)
+
+    @pl.when(has_above & jnp.logical_not(far_lower))
+    def _():
+        greet((date, strip - 1))
+        greet((mate, strip - 1))
+
+    @pl.when(has_below)
+    def _():
+        greet((date, strip + 1))
+        greet((mate, strip + 1))
+
+    for device in (*partners.values(), onward):
+        greet((device, strip))
 
     loads = []
     for n, (src, dst) in enumerate(
@@ -483,24 +515,6 @@
     ):
         loads.append(pltpu.make_async_copy(src, dst, load_sem.at[n]))
         loads[-1].start()
-
-    barrier = pltpu.get_barrier_semaphore()
-
-    def greet(device):
-        pl.semaphore_signal(barrier, inc=1, device_id=device, device_id_type=MESH)
-
-    @pl.when(has_above & jnp.logical_not(far_lower & upper_asks))
-    def _():
-        greet((date, strip - 1))
-        greet((mate, strip - 1))
-
-    @pl.when(has_below & jnp.logical_not(far_upper & upper_answers))
-    def _():
-        greet((date, strip + 1))
-        greet((mate, strip + 1))
-
-    for device in (*partners.values(), onward):
-        greet((device, strip))
 
     loads[0].wait()
     for i in range(2):
@@ -555,7 +569,7 @@
         remote(own.at[:, :, last_rows], own.at[:, :, top], halo_send.at[1], halo_recv.at[1], (date, strip + 1)),
         remote(own.at[:, :, last_rows], other.at[0, :, :, top], halo_send.at[3], halo_recv.at[3], (mate, strip + 1)),
     ]
-    inside = has_above & has_below & jnp.logical_not(asks)
+    inside = has_above & has_below & jnp.logical_not(far_upper)
 
     @pl.when(inside)
     def _():
@@ -565,25 +579,20 @@
     def _():
         pl.semaphore_wait(barrier, 7)
 
-    @pl.when(has_above & jnp.logical_not(far_lower & asks))
+    @pl.when(far_lower)
+    def _():
+        for device in (date, mate):
+            pl.semaphore_signal(far_sem, inc=1, device_id=(device, strip - 1), device_id_type=MESH)
+
+    @pl.when(has_above)
     def _():
         for copy in up:
             copy.start()
 
-    @pl.when(has_below & jnp.logical_not(far_upper & asks))
+    @pl.when(has_below & jnp.logical_not(far_upper))
     def _():
         for copy in down:
             copy.start()
-
-    @pl.when(far_lower & upper_asks)
-    def _():
-        for device in (date, mate):
-            pl.semaphore_signal(far_sem, inc=1, device_id=(device, strip - 1), device_id_type=MESH)
-
-    @pl.when(far_upper & upper_answers)
-    def _():
-        for device in (date, mate):
-            pl.semaphore_signal(far_sem, inc=1, device_id=(device, strip + 1), device_id_type=MESH)
 
     mains = {}
     for i in range(2):
@@ -648,19 +657,9 @@
                 widen(i, q)
 
     def send_far():
-        @pl.when(asks)
-        def _():
-            pl.semaphore_wait(far_sem, 2)
-
-        @pl.when(far_upper & asks)
-        def _():
-            for copy in down:
-                copy.start()
-
-        @pl.when(far_lower & asks)
-        def _():
-            for copy in up:
-                copy.start()
+        pl.semaphore_wait(far_sem, 2)
+        for copy in down:
+            copy.start()
 
     def before_look(turn):
         @pl.when(turn == 0)
@@ -682,7 +681,10 @@
                     mains[1, i, c].wait_recv()
                     forwards[i, c].start()
                 if i == 0:
-                    send_far()
+
+                    @pl.when(far_upper)
+                    def _():
+                        send_far()
 
         @pl.when(turn == 2)
         def _():
@@ -730,7 +732,7 @@
 
     tables = (box_t, forward_t, inverse_t, near_t, same_t)
     compute_all(
-        strip * ROWS, partner, valid, own32, other, tables, coherence, filtered, work, before_look, before_halo, after
+        strip * ROWS, partner, valid, own32, other, tables, coherence, filtered, work, before_look, before_halo, after,
     )
 
     @pl.when(has_above)

time: 28.9 us -> 27.7 us (0.958)
  the two profiles are of different devices: /device:TPU:88 before, /device:TPU:224 now
where the time goes in v4:
time: 27.7 us; the launch traced here: 27.5 us
  Pallas kernels  26.9 us (97%)
  between operations  0.64 us (2%)
    pallas_call x1, Pallas kernels, exchange(): pl.pallas_call(exchange_kernel, out_shape=(jax.ShapeDtypeStruct((4, 2, 4,...  24 us
    pallas_call x1, Pallas kernels, hand_on(): pl.pallas_call(hand_on_kernel, out_shape=(jax.ShapeDtypeStruct(coherence....  2.89 us

profile of v4, /device:TPU:224, one launch (start us, length us, event | category | flops | bytes accessed | tf_op | source)
XLA Modules:
  0.0 27.5 jit_solution(13154448154090711839)
XLA Ops:
  0.6 24.0 %interferograms.1 = (f32[4,2,4,64,128]{4,3,2,1,0:T(8,128)}, f32[4,2,2,4,64,128]{5,4,3,2,1,0:T(8,128)}) custom-call(s32[1,2,4]{2,1,0:T(2,128)} %bitcast.13, s32[2,2,4]{2,1,0:T(2,128)} %bitcast.12, bf16[2,2,32,1024]{3,2,1,0:T(8,128)(2,1)} %slc_hbm.1, bf16[256,256]{1,0:T(8,128)(2,1)} %constant.10.clone.box_h, bf16[768,256]{1,0:T(8,128)(2,1)} %constant.11.clone.forward_h, ...), custom_call_target="tpu_custom_call" | custom-call | tf_op jit(solution)/shard_map/interferograms/pallas_call | solution.py:758
  24.7 2.9 %hand_on.1 = (f32[4,2,4,64,128]{4,3,2,1,0:T(8,128)}, f32[4,2,2,4,64,128]{5,4,3,2,1,0:T(8,128)}) custom-call(f32[4,2,4,64,128]{4,3,2,1,0:T(8,128)} %get-tuple-element.6.done_coherence, f32[4,2,2,4,64,128]{5,4,3,2,1,0:T(8,128)} %get-tuple-element.7.done_filtered), custom_call_target="tpu_custom_call" | custom-call | tf_op jit(solution)/shard_map/hand_on/pallas_call | solution.py:820

commit v5 on v4

--- a/solution.py
+++ b/solution.py
@@ -430,7 +430,7 @@
         after(turn)
 
     def step(n, carry):
-        looks = (n < turns - 1) | (n == turns + 1)
+        looks = (n < turns - 1) | (n == turns)
 
         @pl.when(looks)
         def _():
@@ -595,9 +595,9 @@
             copy.start()
 
     mains = {}
-    for i in range(2):
-        for c in range(2):
-            for n, r in enumerate((1, 3, 0)):
+    for n, r in enumerate((1, 3, 0)):
+        for i in range(2):
+            for c in range(2):
                 mains[r, i, c] = remote(
                     own.at[i, c, body],
                     other.at[r, i, c, body],

time: 27.7 us -> 27.3 us (0.986)
  Pallas kernels: 26.9 us -> 26.6 us
    pallas_call x1, Pallas kernels: 24 us -> 23.7 us  [exchange(): pl.pallas_call(exchange_kernel, out_shape=(jax.ShapeDtypeStruct((4, 2, 4,...]
where the time goes in v5:
time: 27.3 us; the launch traced here: 27.2 us
  Pallas kernels  26.6 us (97%)
  between operations  0.64 us (2%)
    pallas_call x1, Pallas kernels, exchange(): pl.pallas_call(exchange_kernel, out_shape=(jax.ShapeDtypeStruct((4, 2, 4,...  23.7 us
    pallas_call x1, Pallas kernels, hand_on(): pl.pallas_call(hand_on_kernel, out_shape=(jax.ShapeDtypeStruct(coherence....  2.89 us

profile of v5, /device:TPU:224, one launch (start us, length us, event | category | flops | bytes accessed | tf_op | source)
XLA Modules:
  0.0 27.2 jit_solution(5779350370309302244)
XLA Ops:
  0.6 23.7 %interferograms.1 = (f32[4,2,4,64,128]{4,3,2,1,0:T(8,128)}, f32[4,2,2,4,64,128]{5,4,3,2,1,0:T(8,128)}) custom-call(s32[1,2,4]{2,1,0:T(2,128)} %bitcast.13, s32[2,2,4]{2,1,0:T(2,128)} %bitcast.12, bf16[2,2,32,1024]{3,2,1,0:T(8,128)(2,1)} %slc_hbm.1, bf16[256,256]{1,0:T(8,128)(2,1)} %constant.10.clone.box_h, bf16[768,256]{1,0:T(8,128)(2,1)} %constant.11.clone.forward_h, ...), custom_call_target="tpu_custom_call" | custom-call | tf_op jit(solution)/shard_map/interferograms/pallas_call | solution.py:758
  24.3 2.9 %hand_on.1 = (f32[4,2,4,64,128]{4,3,2,1,0:T(8,128)}, f32[4,2,2,4,64,128]{5,4,3,2,1,0:T(8,128)}) custom-call(f32[4,2,4,64,128]{4,3,2,1,0:T(8,128)} %get-tuple-element.6.done_coherence, f32[4,2,2,4,64,128]{5,4,3,2,1,0:T(8,128)} %get-tuple-element.7.done_filtered), custom_call_target="tpu_custom_call" | custom-call | tf_op jit(solution)/shard_map/hand_on/pallas_call | solution.py:820

commit v6 on v4

--- a/solution.py
+++ b/solution.py
@@ -430,7 +430,7 @@
         after(turn)
 
     def step(n, carry):
-        looks = (n < turns - 1) | (n == turns + 1)
+        looks = (n < turns - 1) | (n == turns)
 
         @pl.when(looks)
         def _():
@@ -463,7 +463,7 @@
     coherence_hbm, filtered_hbm,
     own32, other, coherence, filtered, box_t, forward_t, inverse_t, near_t, same_t,
     slc, own, lines, partner, valid, load_sem, out_sem,
-    far_sem, halo_send, halo_recv, main_send, main_recv, edge_send, edge_recv, fwd_send, fwd_recv, *work,
+    far_sem, halo_send, halo_recv, piece_send, piece_recv, main_send, main_recv, edge_send, edge_recv, fwd_send, fwd_recv, *work,
 ):
     date = lax.axis_index("date")
     strip = lax.axis_index("strip")
@@ -594,15 +594,25 @@
         for copy in down:
             copy.start()
 
-    mains = {}
+    mains, pieces = {}, {}
+    halves = [pl.ds(EDGE + h * (BODY // 2), BODY // 2) for h in range(2)]
     for i in range(2):
         for c in range(2):
-            for n, r in enumerate((1, 3, 0)):
+            for h, at in enumerate(halves):
+                pieces[i, c, h] = remote(
+                    own.at[i, c, at],
+                    other.at[1, i, c, at],
+                    piece_send.at[i, c, h],
+                    piece_recv.at[i, c, h],
+                    (partners[1], strip),
+                )
+                pieces[i, c, h].start()
+            for n, r in ((1, 3), (2, 0)):
                 mains[r, i, c] = remote(
                     own.at[i, c, body],
                     other.at[r, i, c, body],
-                    main_send.at[n, i, c],
-                    main_recv.at[n, i, c],
+                    main_send.at[n - 1, i, c],
+                    main_recv.at[n - 1, i, c],
                     (partners[r], strip),
                 )
                 mains[r, i, c].start()
@@ -622,13 +632,14 @@
     forwards, edges = {}, {}
     for i in range(2):
         for c in range(2):
-            forwards[i, c] = remote(
-                other.at[1, i, c, body],
-                other.at[2, i, c, body],
-                fwd_send.at[i, c],
-                fwd_recv.at[i, c],
-                (onward, strip),
-            )
+            for h, at in enumerate(halves):
+                forwards[i, c, h] = remote(
+                    other.at[1, i, c, at],
+                    other.at[2, i, c, at],
+                    fwd_send.at[i, c, h],
+                    fwd_recv.at[i, c, h],
+                    (onward, strip),
+                )
     for n, r in enumerate((1, 2, 3)):
         for side, at in enumerate((top, bottom)):
             edges[r, side] = remote(
@@ -678,8 +689,9 @@
 
             for i in range(2):
                 for c in range(2):
-                    mains[1, i, c].wait_recv()
-                    forwards[i, c].start()
+                    for h in range(2):
+                        pieces[i, c, h].wait_recv()
+                        forwards[i, c, h].start()
                 if i == 0:
 
                     @pl.when(far_upper)
@@ -745,7 +757,7 @@
         for copy in down:
             copy.wait_send()
 
-    for copy in (*mains.values(), *edges.values(), *forwards.values()):
+    for copy in (*pieces.values(), *mains.values(), *edges.values(), *forwards.values()):
         copy.wait_send()
     for turn in range(4):
         for copy in outputs(jnp.int32(turn)):
@@ -781,12 +793,14 @@
             pltpu.SemaphoreType.REGULAR,
             dma((4,)),
             dma((4,)),
-            dma((3, 2, 2)),
-            dma((3, 2, 2)),
+            dma((2, 2, 2)),
+            dma((2, 2, 2)),
+            dma((2, 2, 2)),
+            dma((2, 2, 2)),
             dma((3, 2)),
             dma((3, 2)),
-            dma((2, 2)),
-            dma((2, 2)),
+            dma((2, 2, 2)),
+            dma((2, 2, 2)),
         ]
         + work_shapes(),
         compiler_params=pltpu.CompilerParams(

time: 27.7 us -> 27.1 us (0.978)
  Pallas kernels: 26.9 us -> 26.3 us
    pallas_call x1, Pallas kernels: 24 us -> 23.4 us  [exchange(): pl.pallas_call(exchange_kernel, out_shape=(jax.ShapeDtypeStruct((4, 2, 4,...]
where the time goes in v6:
time: 27.1 us; the launch traced here: 26.9 us
  Pallas kernels  26.3 us (97%)
  between operations  0.64 us (2%)
    pallas_call x1, Pallas kernels, exchange(): pl.pallas_call(exchange_kernel, out_shape=(jax.ShapeDtypeStruct((4, 2, 4,...  23.4 us
    pallas_call x1, Pallas kernels, hand_on(): pl.pallas_call(hand_on_kernel, out_shape=(jax.ShapeDtypeStruct(coherence....  2.89 us

profile of v6, /device:TPU:224, one launch (start us, length us, event | category | flops | bytes accessed | tf_op | source)
XLA Modules:
  0.0 26.9 jit_solution(868443720655897167)
XLA Ops:
  0.6 23.4 %interferograms.1 = (f32[4,2,4,64,128]{4,3,2,1,0:T(8,128)}, f32[4,2,2,4,64,128]{5,4,3,2,1,0:T(8,128)}) custom-call(s32[1,2,4]{2,1,0:T(2,128)} %bitcast.13, s32[2,2,4]{2,1,0:T(2,128)} %bitcast.12, bf16[2,2,32,1024]{3,2,1,0:T(8,128)(2,1)} %slc_hbm.1, bf16[256,256]{1,0:T(8,128)(2,1)} %constant.10.clone.box_h, bf16[768,256]{1,0:T(8,128)(2,1)} %constant.11.clone.forward_h, ...), custom_call_target="tpu_custom_call" | custom-call | tf_op jit(solution)/shard_map/interferograms/pallas_call | solution.py:770
  24.1 2.9 %hand_on.1 = (f32[4,2,4,64,128]{4,3,2,1,0:T(8,128)}, f32[4,2,2,4,64,128]{5,4,3,2,1,0:T(8,128)}) custom-call(f32[4,2,4,64,128]{4,3,2,1,0:T(8,128)} %get-tuple-element.6.done_coherence, f32[4,2,2,4,64,128]{5,4,3,2,1,0:T(8,128)} %get-tuple-element.7.done_filtered), custom_call_target="tpu_custom_call" | custom-call | tf_op jit(solution)/shard_map/hand_on/pallas_call | solution.py:834

commit v7 on v6

--- a/solution.py
+++ b/solution.py
@@ -417,6 +417,7 @@
 
     def filter_turn(turn):
         halo_turn(turn)
+        after(turn, 0)
         rnd = place_of(turn)
         together(
             [
@@ -427,7 +428,7 @@
                 for i in range(2)
             ]
         )
-        after(turn)
+        after(turn, 1)
 
     def step(n, carry):
         looks = (n < turns - 1) | (n == turns)
@@ -738,9 +739,8 @@
             pltpu.make_async_copy(filtered.at[rnd], filtered_hbm.at[rnd], out_sem.at[1, turn]),
         ]
 
-    def after(turn):
-        for copy in outputs(turn):
-            copy.start()
+    def after(turn, n):
+        outputs(turn)[n].start()
 
     tables = (box_t, forward_t, inverse_t, near_t, same_t)
     compute_all(

time: 27.1 us -> 27.1 us (level)
  no operation moved by 1% of the time
where the time goes in v7:
time: 27.1 us; the launch traced here: 26.9 us
  Pallas kernels  26.3 us (97%)
  between operations  0.64 us (2%)
    pallas_call x1, Pallas kernels, exchange(): pl.pallas_call(exchange_kernel, out_shape=(jax.ShapeDtypeStruct((4, 2, 4,...  23.4 us
    pallas_call x1, Pallas kernels, hand_on(): pl.pallas_call(hand_on_kernel, out_shape=(jax.ShapeDtypeStruct(coherence....  2.89 us

profile of v7, /device:TPU:224, one launch (start us, length us, event | category | flops | bytes accessed | tf_op | source)
XLA Modules:
  0.0 26.9 jit_solution(868443720655897167)
XLA Ops:
  0.6 23.4 %interferograms.1 = (f32[4,2,4,64,128]{4,3,2,1,0:T(8,128)}, f32[4,2,2,4,64,128]{5,4,3,2,1,0:T(8,128)}) custom-call(s32[1,2,4]{2,1,0:T(2,128)} %bitcast.13, s32[2,2,4]{2,1,0:T(2,128)} %bitcast.12, bf16[2,2,32,1024]{3,2,1,0:T(8,128)(2,1)} %slc_hbm.1, bf16[256,256]{1,0:T(8,128)(2,1)} %constant.10.clone.box_h, bf16[768,256]{1,0:T(8,128)(2,1)} %constant.11.clone.forward_h, ...), custom_call_target="tpu_custom_call" | custom-call | tf_op jit(solution)/shard_map/interferograms/pallas_call | solution.py:770
  24.1 2.9 %hand_on.1 = (f32[4,2,4,64,128]{4,3,2,1,0:T(8,128)}, f32[4,2,2,4,64,128]{5,4,3,2,1,0:T(8,128)}) custom-call(f32[4,2,4,64,128]{4,3,2,1,0:T(8,128)} %get-tuple-element.6.done_coherence, f32[4,2,2,4,64,128]{5,4,3,2,1,0:T(8,128)} %get-tuple-element.7.done_filtered), custom_call_target="tpu_custom_call" | custom-call | tf_op jit(solution)/shard_map/hand_on/pallas_call | solution.py:834
